TPU v7x, 512 devices: a whole 4x8x8 slice. The times are simulated.
512 devices in a mesh: gx: 64 (over z, y), gy: 8 (over x, core).
Axes of the slice: x: 4, y: 8, z: 8, core: 2. Of those that a mesh axis runs over, the one named last changes fastest.
Arguments:
- points_x: bfloat16 [262144, 128], P('gx'), may hold values from -40 to 40
- points_y: bfloat16 [65536, 128], P('gy'), may hold values from -1.5 to 1.5
- g_init: float32 [65536], P('gy'), may hold values from -4 to 4
- log_a: float32 [262144], P('gx'), may hold values from -1 to 1
- log_b: float32 [65536], P('gy'), may hold values from -1 to 1
- tile_cols: int32 [512, 16], P('gx'), may hold values from 0 to 127, as said below
- tile_counts: int32 [512], P('gx'), may hold values from 2 to 16, as said below
Outputs:
- row_potential: float32 [262144], P('gx')
- column_potential: float32 [65536], P('gy')
- barycenter: float32 [262144, 128], P('gx')
Inputs may be any that keep to these rules, and one draw needn't show every extreme that they name: `tile_cols`: each tile row lists 16 different column tiles; every column tile is the first entry of some tile row. `tile_counts`: some tile row keeps all 16.
All inputs are finite; a program needn't handle non-finite values.
Results may differ from a plain program's by a relative error of at most 0.0034.
Values sent between devices are 32-bit elements; how exact they have to be, the bound alone decides.
A program may use at most 64 MiB of HBM per device.

v0:
```python
import jax
import jax.numpy as jnp
from jax import lax
from jax.sharding import PartitionSpec as P

TILE = 512


EPSILON = 0.5
INV_EPS = 2.0
NEG_FILL = -1e30


def merged(value, axis, join):
    pieces = jax.tree.map(lambda part: lax.all_gather(part, axis), value)
    head = jax.tree.map(lambda part: part[0], pieces)
    tail = jax.tree.map(lambda part: part[1:], pieces)
    running, _ = lax.scan(lambda running, share: (join(running, share), None), head, tail)
    return running


def merge_pair(left, right):
    peak = jnp.maximum(left[0], right[0])
    return (peak, left[1] * jnp.exp(left[0] - peak) + right[1] * jnp.exp(right[0] - peak))


def local(points_x, points_y, g_init, log_a, log_b, tile_cols, tile_counts):
    row_tiles, most = tile_cols.shape
    col_tiles = points_y.shape[0] // TILE
    width = points_x.shape[1]
    column_index = lax.axis_index("gy")
    slot_ids = jnp.arange(most, dtype=jnp.int32)
    owned_mask = (tile_cols // col_tiles == column_index) & (
        slot_ids[None, :] < tile_counts[:, None]
    )
    flat_flags = owned_mask.reshape(-1).astype(jnp.int32)
    positions = jnp.cumsum(flat_flags) - 1
    live_tiles = jnp.sum(flat_flags)
    capacity = row_tiles * most
    targets = jnp.where(flat_flags > 0, positions, capacity)
    row_source = jnp.broadcast_to(
        jnp.arange(row_tiles, dtype=jnp.int32)[:, None], (row_tiles, most)
    ).reshape(-1)
    list_rows = jnp.zeros((capacity,), jnp.int32).at[targets].set(row_source, mode="drop")
    list_cols = (
        jnp.zeros((capacity,), jnp.int32)
        .at[targets]
        .set((tile_cols % col_tiles).reshape(-1), mode="drop")
    )
    g_start = g_init.reshape(col_tiles, TILE)

    def tile_pair(step):
        row_at = list_rows[step]
        col_at = list_cols[step]
        x_tile = lax.dynamic_slice_in_dim(points_x, row_at * TILE, TILE, 0)
        y_tile = lax.dynamic_slice_in_dim(points_y, col_at * TILE, TILE, 0)
        dots = lax.dot_general(
            x_tile, y_tile, (((1,), (1,)), ((), ())), preferred_element_type=jnp.float32
        )
        return (row_at, col_at, y_tile, dots)

    def row_step(step, carry):
        peak_rows, mass_rows = carry
        row_at, col_at, y_tile, dots = tile_pair(step)
        logits = (g_start[col_at][None, :] + dots) * INV_EPS
        tile_peak = jnp.max(logits, axis=1)
        tile_mass = jnp.sum(jnp.exp(logits - tile_peak[:, None]), axis=1)
        peak, mass = merge_pair((peak_rows[row_at], mass_rows[row_at]), (tile_peak, tile_mass))
        return (peak_rows.at[row_at].set(peak), mass_rows.at[row_at].set(mass))

    empty_rows = (
        jnp.full((row_tiles, TILE), NEG_FILL, jnp.float32),
        jnp.zeros((row_tiles, TILE), jnp.float32),
    )
    peak_rows, mass_rows = lax.fori_loop(0, live_tiles, row_step, empty_rows)
    peak_rows, mass_rows = merged((peak_rows, mass_rows), "gy", merge_pair)
    f_pot = EPSILON * (log_a.reshape(row_tiles, TILE) - (peak_rows + jnp.log(mass_rows)))

    def column_step(step, carry):
        peak_cols, mass_cols = carry
        row_at, col_at, y_tile, dots = tile_pair(step)
        logits = (f_pot[row_at][:, None] + dots) * INV_EPS
        tile_peak = jnp.max(logits, axis=0)
        tile_mass = jnp.sum(jnp.exp(logits - tile_peak[None, :]), axis=0)
        peak, mass = merge_pair((peak_cols[col_at], mass_cols[col_at]), (tile_peak, tile_mass))
        return (peak_cols.at[col_at].set(peak), mass_cols.at[col_at].set(mass))

    empty_cols = (
        jnp.full((col_tiles, TILE), NEG_FILL, jnp.float32),
        jnp.zeros((col_tiles, TILE), jnp.float32),
    )
    peak_cols, mass_cols = lax.fori_loop(0, live_tiles, column_step, empty_cols)
    peak_cols, mass_cols = merged((peak_cols, mass_cols), "gx", merge_pair)
    g_pot = EPSILON * (log_b.reshape(col_tiles, TILE) - (peak_cols + jnp.log(mass_cols)))

    def bary_step(step, carry):
        numer, denom = carry
        row_at, col_at, y_tile, dots = tile_pair(step)
        weights = jnp.exp((f_pot[row_at][:, None] + g_pot[col_at][None, :] + dots) * INV_EPS)
        product = jnp.dot(weights.astype(jnp.bfloat16), y_tile, preferred_element_type=jnp.float32)
        before = lax.dynamic_slice_in_dim(numer, row_at * TILE, TILE, 0)
        numer = lax.dynamic_update_slice_in_dim(numer, before + product, row_at * TILE, 0)
        return (numer, denom.at[row_at].add(jnp.sum(weights, axis=1)))

    empty_bary = (
        jnp.zeros((row_tiles * TILE, width), jnp.float32),
        jnp.zeros((row_tiles, TILE), jnp.float32),
    )
    numer, denom = lax.fori_loop(0, live_tiles, bary_step, empty_bary)
    total_numer, total_denom = lax.psum((numer, denom.reshape(-1)), "gy")
    barycenter = total_numer / total_denom[:, None]
    return (f_pot.reshape(-1), g_pot.reshape(-1), barycenter)


def solution(mesh):
    in_specs = (P("gx", None), P("gy", None), P("gy"), P("gx"), P("gy"), P("gx", None), P("gx"))
    out_specs = (P("gx"), P("gy"), P("gx", None))
    return jax.shard_map(local, mesh=mesh, in_specs=in_specs, out_specs=out_specs, check_vma=False)
```

profile of v0, /device:TPU:1, one launch (start us, length us, event | category | flops | bytes accessed | tf_op | source)
XLA Modules:
  0.0 952.7 jit_solution(17627506378115961067)
XLA Ops:
  7.3 1.4 fusion.31
  12.0 59.8 %while.65 = (s32[]{:T(128)}, f32[8,512]{1,0:T(8,128)S(1)}, f32[8,512]{1,0:T(8,128)S(1)}, s32[]{:T(128)}, s32[128]{0:T(128)S(1)}, /*index=5*/s32[128]{0:T(128)S(1...) while((s32[]{:T(128)}, f32[8,512]{1,0:T(8,128)S(1)}, ...), condition=%wide.region_8.9_spmd, body=%wide.region_4.8_spmd.sunk | while | flops 68422680 | bytes 2392505 | solution.py:75
  18.3 1.4 and_reduce_fusion.6
  28.1 1.4 and_reduce_fusion.6
  38.0 1.4 and_reduce_fusion.6
  47.9 1.4 and_reduce_fusion.6
  57.7 1.4 and_reduce_fusion.6
  67.6 1.4 and_reduce_fusion.6
  71.8 9.9 %all-gather.1 = f32[64,512]{1,0:T(8,128)S(1)} all-gather(f32[8,512]{1,0:T(8,128)S(1)} %get-tuple-element.272), channel_id=3, replica_groups=mesh['gx'=64,'gy'=8] {'gy'}, dimensions={0}, use_global_device_ids=true | all-gather | bytes 147456 | tf_op jit(solution)/shard_map/all_gather | solution.py:15
  81.7 13.1 %all-gather = f32[64,512]{1,0:T(8,128)S(1)} all-gather(f32[8,512]{1,0:T(8,128)S(1)} %get-tuple-element.271), channel_id=2, replica_groups=mesh['gx'=64,'gy'=8] {'gy'}, dimensions={0}, use_global_device_ids=true | all-gather | bytes 147456 | tf_op jit(solution)/shard_map/all_gather | solution.py:15
  95.2 60.7 %while.67 = (s32[]{:T(128)}, f32[16,512]{1,0:T(8,128)S(1)}, f32[16,512]{1,0:T(8,128)S(1)}, s32[]{:T(128)}, s32[128]{0:T(128)S(1)}, /*index=5*/s32[128]{0:T(128)S...) while((s32[]{:T(128)}, f32[16,512]{1,0:T(8,128)S(1)}, ...), condition=%wide.region_15.16_spmd, body=%wide.region_11.15_spmd.sunk | while | flops 68422680 | bytes 2392505 | solution.py:92
  157.4 356.7 %all-gather.7.cloned.1.call-done = f32[1024,512]{1,0:T(8,128)} async-done(((f32[16,512]{1,0:T(8,128)}), f32[1024,512]{1,0:T(8,128)}) %all-gather.7.cloned.1.call-update) | async-done | bytes 2097168 | tf_op jit(solution)/shard_map/all_gather | solution.py:15
  514.8 83.4 %all-gather.9.cloned.1.call-done = f32[1024,512]{1,0:T(8,128)} async-done(((f32[16,512]{1,0:T(8,128)}), f32[1024,512]{1,0:T(8,128)}) %all-gather.9.cloned.1.call-update) | async-done | bytes 2097168 | tf_op jit(solution)/shard_map/all_gather | solution.py:15
  598.2 3.1 slice.117
  601.3 51.4 %while.68 = (s32[]{:T(128)}, f32[16,512]{1,0:T(8,128)S(1)}, f32[16,512]{1,0:T(8,128)S(1)}, f32[63,16,512]{2,1,0:T(8,128)S(1)}, f32[63,16,512]{2,1,0:T(8,128)}, /*index=5*/s32[]{:T(128)}) while((s32[]{:T(128)}, f32[16,512]{1,0:T(8,128)S(1)}, f32[16,512]{1,0:T(8,128)S(1)}, f32[63,16,512]{2,1,0:T(8,128)S(1)}, f32[63,16,512]{2,1,0:T(8,128)}, ...), condition=%wide.region_17.18_spmd, body=%wide.region_16.17_spmd.sunk | while | flops 49154 | bytes 196689 | solution.py:18
  652.8 67.1 %while.69 = (s32[]{:T(128)}, f32[4096,128]{1,0:T(8,128)S(1)}, f32[8,512]{1,0:T(8,128)S(1)}, s32[]{:T(128)}, s32[128]{0:T(128)S(1)}, /*index=5*/f32[8,512]{1,0:T(...) while((s32[]{:T(128)}, f32[4096,128]{1,0:T(8,128)S(1)}, ...), condition=%wide.region_21.22_spmd, body=%wide.region_18.21_spmd.sunk | while | flops 135594528 | bytes 1991113 | solution.py:109
  660.6 1.4 fusion.51
  671.6 1.4 fusion.51
  682.7 1.4 fusion.51
  693.8 1.4 fusion.51
  716.0 1.4 fusion.51
  722.5 20.4 %psum.15 = f32[4096]{0:T(1024)S(1)} all-reduce(f32[4096]{0:T(1024)S(1)} %bitcast.110), channel_id=1, replica_groups=mesh['gx'=64,'gy'=8] {'gy'}, use_global_device_ids=true, to_apply=%region_23.24 | all-reduce | flops 4096 | bytes 32768 | tf_op jit(solution)/shard_map/psum | solution.py:110
  742.9 200.3 %all-reduce.2.cloned.1.call-done = f32[4096,128]{1,0:T(8,128)} async-done(((f32[4096,128]{1,0:T(8,128)}), f32[4096,128]{1,0:T(8,128)}) %all-reduce.2.cloned.1.call-update) | async-done | bytes 2097168 | tf_op jit(solution)/shard_map/psum | solution.py:110
  943.3 2.9 broadcast_divide_fusion
  (267 shorter events, 128.8 us)
Async XLA Ops:
  7.2 506.9 %all-gather.7.cloned.1.call-start = ((), (), s32[]{:S(2)}) async-start(), calls=%async_computation.1 | async-start | bytes 2129920 | tf_op jit(solution)/shard_map/all_gather | solution.py:15
  11.9 82.8 %copy-start.5 = (f32[4096]{0:T(1024)S(1)}, f32[4096]{0:T(1024)}, u32[]{:S(2)}) copy-start(f32[4096]{0:T(1024)} %param.30) | copy-start | bytes 49156
  11.9 83.2 %copy-start.6 = (s32[2]{0:T(128)S(1)}, s32[2]{0:T(128)}, u32[]{:S(2)}) copy-start(s32[2]{0:T(128)} %constant.205.clone.1) | copy-start | bytes 28
  95.2 62.2 %copy-start.4 = (f32[8192]{0:T(1024)S(1)}, f32[8192]{0:T(1024)}, u32[]{:S(2)}) copy-start(f32[8192]{0:T(1024)} %param.31) | copy-start | bytes 98308
  155.9 0.6 copy-start.1
  155.9 0.7 copy-start.2
  156.5 441.7 %all-gather.9.cloned.1.call-start = ((), (), s32[]{:S(2)}) async-start(), calls=%async_computation.2 | async-start | bytes 2129920 | tf_op jit(solution)/shard_map/all_gather | solution.py:15
  157.3 786.0 %all-reduce.2.cloned.1.call-start = ((), (), s32[]{:S(2)}) async-start(), calls=%async_computation | async-start | bytes 4194304 | tf_op jit(solution)/shard_map/psum | solution.py:110
  514.8 86.5 %slice-start = ((f32[1024,512]{1,0:T(8,128)}), f32[1008,512]{1,0:T(8,128)S(1)}, s32[]{:S(2)}) async-start(f32[1024,512]{1,0:T(8,128)} %all-gather.7.cloned.1.call-done), calls=%async_computation.3 | async-start | bytes 4128768 | tf_op jit(solution)/shard_map/slice | solution.py:17
  598.2 3.1 slice-start.1
  601.3 51.6 %copy-start.3 = (s32[2]{0:T(128)S(1)}, s32[2]{0:T(128)}, u32[]{:S(2)}) copy-start(s32[2]{0:T(128)} %get-tuple-element.875) | copy-start | bytes 28
  720.0 1.3 copy-start
Sparse Core Ops, SparseCore 0:
  156.7 357.3 all-gather.6
  517.7 80.4 all-gather.8
  721.4 221.7 all-reduce.1
where the time goes:
time: 965 us; the launch traced here: 953 us
  waiting for transfers between devices  641 us (66%)
  loops' own time  104 us (11%)
  other arithmetic  85.7 us (9%)
  blocking collectives  43.3 us (4%)
  local copies, waits for them, and re-layouts  33.2 us (3%)
  matrix products  31.1 us (3%)
  between operations  14 us (1%)
    all_gather x2, waiting for transfers between devices, merged(): pieces = jax.tree.map(lambda part: lax.all_gather(part, axis), value)  440 us
    psum x1, waiting for transfers between devices, local(): total_numer, total_denom = lax.psum((numer, denom.reshape(-1)), 'gy')  200 us
    add x70, other arithmetic, merge_pair(): left[1] * jnp.exp(left[0] - peak) + right[1] * jnp.exp(right[0] - peak)  50.6 us
    another operation x1, loops' own time, local(): numer, denom = lax.fori_loop(0, live_tiles, bary_step, empty_bary)  35.7 us
    another operation x1, loops' own time, local(): peak_cols, mass_cols = lax.fori_loop(0, live_tiles, column_step, empty_cols)  35.7 us
    another operation x1, loops' own time, local(): peak_rows, mass_rows = lax.fori_loop(0, live_tiles, row_step, empty_rows)  31.6 us
    another operation x37, other arithmetic  28.3 us
    dot_general x18, matrix products, tile_pair(): lax.dot_general(x_tile, y_tile, (((1,), (1,)), ((), ())), preferred_eleme...  23.5 us
  transfers between devices with their start and end apart: 3, of which 3 were waited for; matrix products, arithmetic and copies ran while one was open for 0% of the time, Pallas kernels for 0%

commit v1 on v0

v1 whole, which is shorter than its diff:
```python
import functools

import jax
import jax.numpy as jnp
from jax import lax
from jax.experimental import pallas as pl
from jax.experimental.pallas import tpu as pltpu
from jax.sharding import PartitionSpec as P

TILE = 512
LANES = 128
CHUNKS = TILE // LANES
MESH = pl.DeviceIdType.MESH
NEG_FILL = -1e30
SCALE = 2.8853900817779268
VMEM = pl.BlockSpec(memory_space=pltpu.VMEM)
SMEM = pl.BlockSpec(memory_space=pltpu.SMEM)
VMEM_LIMIT = 40 * 1024 * 1024


def params(**kw):
    return pltpu.CompilerParams(vmem_limit_bytes=VMEM_LIMIT, **kw)


def split3(value):
    high = value.astype(jnp.bfloat16).astype(jnp.float32)
    rest = value - high
    middle = rest.astype(jnp.bfloat16).astype(jnp.float32)
    low = (rest - middle).astype(jnp.bfloat16).astype(jnp.float32)
    return [high, middle, low]


def tile_rows(ref, tiles):
    return jnp.concatenate(
        [ref[pl.ds(q, tiles, stride=CHUNKS), :] for q in range(CHUNKS)], axis=1
    )


def as_columns(pieces):
    rows = sum(piece.shape[0] for piece in pieces)
    pieces = pieces + [jnp.zeros((LANES - rows, TILE), jnp.float32)]
    return jnp.concatenate(pieces, axis=0).T.astype(jnp.bfloat16)


def lane_mask(first, period, which):
    lane = lax.broadcasted_iota(jnp.int32, (1, LANES), 1) - first
    hit = (lane == which) | (lane == which + period) | (lane == which + 2 * period)
    return jnp.where(hit, 1.0, 0.0)


def spread(row):
    return jnp.broadcast_to(row, (TILE, LANES)).astype(jnp.bfloat16)


def tile_at(ref, index):
    return ref[pl.ds(pl.multiple_of(index * TILE, TILE), TILE), :]


def product(left, right):
    return lax.dot_general(
        left, right, (((1,), (1,)), ((), ())), preferred_element_type=jnp.float32
    )


def lse_pass(list_ref, live, pick, outer_ref, inner_ref, pot_tiles, columns, peak, mass):
    peak[...] = jnp.full_like(peak, NEG_FILL)
    mass[...] = jnp.zeros_like(mass)

    def step(at, carry):
        outer, inner = pick(list_ref[at])
        left = jnp.concatenate([tile_at(outer_ref, outer), columns[...]], axis=1)
        right = jnp.concatenate(
            [tile_at(inner_ref, inner), spread(lane_mask(0, pot_tiles, outer))], axis=1
        )
        half = TILE // 2
        for part in range(2):
            lanes = slice(part * half, (part + 1) * half)
            sums = product(left, right[lanes, :]).reshape(TILE // 8, 8, half)
            before = peak[inner, :, lanes]
            top = jnp.maximum(before, jnp.max(sums, axis=0))
            terms = jnp.sum(jnp.exp2((sums - top[None]) * SCALE), axis=0)
            mass[inner, :, lanes] = mass[inner, :, lanes] * jnp.exp2((before - top) * SCALE) + terms
            peak[inner, :, lanes] = top
        return carry

    lax.fori_loop(0, live, step, 0)


def lse_finish(peak, mass, out_ref):
    for tile in range(peak.shape[0]):
        top = jnp.max(peak[tile], axis=0, keepdims=True)
        total = jnp.sum(mass[tile] * jnp.exp2((peak[tile] - top) * SCALE), axis=0, keepdims=True)
        lse = jnp.where(total > 0.0, 2.0 * top + jnp.log(total), NEG_FILL)
        for q in range(CHUNKS):
            out_ref[pl.ds(tile * CHUNKS + q, 1), :] = lse[:, q * LANES : (q + 1) * LANES]


def row_kernel(cols_ref, counts_ref, x_ref, y_ref, g_ref, lse_ref, list_ref, columns, peak, mass):
    row_tiles, most = cols_ref.shape
    col_tiles = y_ref.shape[0] // TILE
    me = lax.axis_index("gy")
    live = jnp.int32(0)
    for row in range(row_tiles):
        count = counts_ref[row]
        for slot in range(most):
            at = cols_ref[row, slot] - me * col_tiles
            owned = (at >= 0) & (at < col_tiles) & (slot < count)
            list_ref[live] = row * col_tiles + at
            live = live + jnp.where(owned, 1, 0)
    list_ref[row_tiles * most] = live
    columns[...] = as_columns(split3(tile_rows(g_ref, col_tiles)))
    pick = lambda pair: (lax.rem(pair, col_tiles), lax.div(pair, col_tiles))
    lse_pass(list_ref, live, pick, y_ref, x_ref, col_tiles, columns, peak, mass)
    lse_finish(peak, mass, lse_ref)


def column_kernel(list_ref, x_ref, y_ref, f_ref, lse_ref, columns, peak, mass):
    row_tiles = x_ref.shape[0] // TILE
    col_tiles = y_ref.shape[0] // TILE
    live = list_ref[list_ref.shape[0] - 1]
    columns[...] = as_columns(split3(tile_rows(f_ref, row_tiles)))
    pick = lambda pair: (lax.div(pair, col_tiles), lax.rem(pair, col_tiles))
    lse_pass(list_ref, live, pick, x_ref, y_ref, row_tiles, columns, peak, mass)
    lse_finish(peak, mass, lse_ref)


def bary_kernel(list_ref, x_ref, y_ref, f_ref, g_ref, out_ref, columns):
    row_tiles = x_ref.shape[0] // TILE
    col_tiles = y_ref.shape[0] // TILE
    width = x_ref.shape[1]
    live = list_ref[list_ref.shape[0] - 1]
    first = 3 * col_tiles
    pots = split3(tile_rows(g_ref, col_tiles)) + split3(tile_rows(f_ref, row_tiles))
    columns[...] = as_columns(pots)
    out_ref[...] = jnp.zeros_like(out_ref)

    def step(at, carry):
        pair = list_ref[at]
        row, col = lax.div(pair, col_tiles), lax.rem(pair, col_tiles)
        lane = lax.broadcasted_iota(jnp.int32, (1, LANES), 1)
        of_g = spread(jnp.where(lane < first, 1.0, 0.0))
        of_f = spread(jnp.where(lane < first, 0.0, 1.0))
        y_tile = tile_at(y_ref, col)
        pot = columns[...]
        left = jnp.concatenate(
            [y_tile, pot * of_g + spread(lane_mask(first, row_tiles, row))], axis=1
        )
        right = jnp.concatenate(
            [tile_at(x_ref, row), pot * of_f + spread(lane_mask(0, col_tiles, col))], axis=1
        )
        half = TILE // 2
        for part in range(2):
            lanes = slice(part * half, (part + 1) * half)
            weights = jnp.exp2(product(left, right[lanes, :]) * SCALE)
            out_ref[row, width:, lanes] += jnp.sum(weights.reshape(TILE // 8, 8, half), axis=0)
            out_ref[row, :width, lanes] += lax.dot_general(
                y_tile,
                weights.astype(jnp.bfloat16),
                (((0,), (0,)), ((), ())),
                preferred_element_type=jnp.float32,
            )
        return carry

    lax.fori_loop(0, live, step, 0)


def meet(peers):
    barrier = pltpu.get_barrier_semaphore()
    for peer in peers:
        pl.semaphore_signal(barrier, inc=1, device_id=peer, device_id_type=MESH)
    pl.semaphore_wait(barrier, len(peers))


def send(src, dst, send_sem, recv_sem, peer):
    copy = pltpu.make_async_remote_copy(
        src_ref=src,
        dst_ref=dst,
        send_sem=send_sem,
        recv_sem=recv_sem,
        device_id=peer,
        device_id_type=MESH,
    )
    copy.start()
    return copy


def join(parts):
    top = parts[0]
    for part in parts[1:]:
        top = jnp.maximum(top, part)
    total = jnp.exp(parts[0] - top)
    for part in parts[1:]:
        total = total + jnp.exp(part - top)
    return top + jnp.log(total)


def row_join_kernel(n, lse_ref, log_a_ref, f_ref, held, send_sem, recv_sem):
    me = lax.axis_index("gy")
    peers = [{"gy": lax.rem(me + d, n)} for d in range(1, n)]
    meet(peers)
    copies = [
        send(lse_ref, held.at[me], send_sem.at[i], recv_sem.at[i], peer)
        for i, peer in enumerate(peers)
    ]
    held[me] = lse_ref[...]
    for copy in copies:
        copy.wait()
    f_ref[...] = 0.5 * (log_a_ref[...] - join([held[k] for k in range(n)]))


def col_join_kernel(
    nz, ny, lse_ref, log_b_ref, g_ref, first, part, second, send_sem, recv_sem
):
    me = lax.axis_index("gx")
    z, y = lax.div(me, ny), lax.rem(me, ny)
    y_places = [lax.rem(y + d, ny) for d in range(1, ny)]
    y_peers = [{"gx": z * ny + at} for at in y_places]
    z_peers = [{"gx": lax.rem(z + d, nz) * ny + y} for d in range(1, nz)]
    meet(y_peers + z_peers)
    copies = [
        send(lse_ref.at[at], first.at[i], send_sem.at[i], recv_sem.at[i], peer)
        for i, (at, peer) in enumerate(zip(y_places, y_peers))
    ]
    for copy in copies:
        copy.wait()
    part[...] = join([lse_ref[y]] + [first[i] for i in range(ny - 1)])
    base = ny - 1
    copies = [
        send(part, second.at[z], send_sem.at[base + i], recv_sem.at[base + i], peer)
        for i, peer in enumerate(z_peers)
    ]
    second[z] = part[...]
    for copy in copies:
        copy.wait()
    g_ref[y] = 0.5 * (log_b_ref[y] - join([second[k] for k in range(nz)]))
    base = ny - 1 + nz - 1
    copies = [
        send(g_ref.at[y], g_ref.at[y], send_sem.at[base + i], recv_sem.at[base + i], peer)
        for i, peer in enumerate(y_peers)
    ]
    for copy in copies:
        copy.wait()


def bary_join_kernel(n, part_ref, out_ref, near, far, send_sem, recv_sem):
    me = lax.axis_index("gy")
    chips = n // 2
    chip, core = lax.div(me, 2), lax.rem(me, 2)
    other = 1 - core
    width = out_ref.shape[1]
    sibling = {"gy": chip * 2 + other}
    places = [lax.rem(chip + d, chips) for d in range(chips)]
    peers = [{"gy": at * 2 + core} for at in places]
    meet([sibling] + peers[1:])

    order = [2, 1, 3, 0]
    inside = {
        d: send(
            part_ref.at[places[d] * 2 + other], near.at[d], send_sem.at[d], recv_sem.at[d], sibling
        )
        for d in order
    }
    across = {}
    for d in order:
        inside[d].wait()
        near[d] = near[d] + part_ref[places[d] * 2 + core]
        if d > 0:
            across[d] = send(
                near.at[d], far.at[d - 1], send_sem.at[4 + d], recv_sem.at[4 + d], peers[d]
            )
    total = near[0]
    for d in (1, 3, 2):
        across[d].wait()
        total = total + far[d - 1]
    ratio = total[:width] / jnp.sum(total[width:], axis=0, keepdims=True)
    mine = out_ref.at[pl.ds(pl.multiple_of(me * TILE, TILE), TILE)]
    mine[...] = ratio.T
    gathered = {
        d: send(mine, mine, send_sem.at[8 + d], recv_sem.at[8 + d], peers[d]) for d in (2, 1, 3)
    }
    handed = [send(mine, mine, send_sem.at[8], recv_sem.at[8], sibling)]
    for d in (1, 3, 2):
        gathered[d].wait()
        source = lax.rem(chip - d + chips, chips) * 2 + core
        block = out_ref.at[pl.ds(pl.multiple_of(source * TILE, TILE), TILE)]
        handed.append(send(block, block, send_sem.at[12 + d], recv_sem.at[12 + d], sibling))
    for copy in handed:
        copy.wait()


def local(gx_size, gy_size, points_x, points_y, g_init, log_a, log_b, tile_cols, tile_counts):
    row_tiles, most = tile_cols.shape
    rows, width = points_x.shape
    cols = points_y.shape[0]
    col_tiles = cols // TILE
    nz = 1
    while nz * nz < gx_size:
        nz *= 2
    ny = gx_size // nz
    f32, i32, bf16 = jnp.float32, jnp.int32, jnp.bfloat16
    row_shape, col_shape = (rows // LANES, LANES), (cols // LANES, LANES)
    block = (cols // LANES // ny, LANES)
    dma = pltpu.SemaphoreType.DMA

    def lse_scratch(tiles):
        return [
            pltpu.VMEM((TILE, LANES), bf16),
            pltpu.VMEM((tiles, 8, TILE), f32),
            pltpu.VMEM((tiles, 8, TILE), f32),
        ]

    row_lse, pairs = pl.pallas_call(
        row_kernel,
        out_shape=(
            jax.ShapeDtypeStruct(row_shape, f32),
            jax.ShapeDtypeStruct((row_tiles * most + 1,), i32),
        ),
        in_specs=[SMEM, SMEM, VMEM, VMEM, VMEM],
        out_specs=(VMEM, SMEM),
        scratch_shapes=lse_scratch(row_tiles),
        compiler_params=params(),
        name="row_pass",
    )(tile_cols, tile_counts, points_x, points_y, g_init.reshape(col_shape))

    f_pot = pl.pallas_call(
        functools.partial(row_join_kernel, gy_size),
        out_shape=jax.ShapeDtypeStruct(row_shape, f32),
        in_specs=[VMEM, VMEM],
        out_specs=VMEM,
        scratch_shapes=[
            pltpu.VMEM((gy_size,) + row_shape, f32),
            dma((gy_size - 1,)),
            dma((gy_size - 1,)),
        ],
        compiler_params=params(collective_id=0, has_side_effects=True),
        name="row_join",
    )(row_lse, log_a.reshape(row_shape))

    col_lse = pl.pallas_call(
        column_kernel,
        out_shape=jax.ShapeDtypeStruct(col_shape, f32),
        in_specs=[SMEM, VMEM, VMEM, VMEM],
        out_specs=VMEM,
        scratch_shapes=lse_scratch(col_tiles),
        compiler_params=params(),
        name="column_pass",
    )(pairs, points_x, points_y, f_pot)

    links = 2 * (ny - 1) + nz - 1
    g_pot = pl.pallas_call(
        functools.partial(col_join_kernel, nz, ny),
        out_shape=jax.ShapeDtypeStruct((ny,) + block, f32),
        in_specs=[VMEM, VMEM],
        out_specs=VMEM,
        scratch_shapes=[
            pltpu.VMEM((ny - 1,) + block, f32),
            pltpu.VMEM(block, f32),
            pltpu.VMEM((nz,) + block, f32),
            dma((links,)),
            dma((links,)),
        ],
        compiler_params=params(collective_id=1, has_side_effects=True),
        name="column_join",
    )(col_lse.reshape((ny,) + block), log_b.reshape((ny,) + block))

    partial = pl.pallas_call(
        bary_kernel,
        out_shape=jax.ShapeDtypeStruct((row_tiles, width + 8, TILE), f32),
        in_specs=[SMEM, VMEM, VMEM, VMEM, VMEM],
        out_specs=VMEM,
        scratch_shapes=[pltpu.VMEM((TILE, LANES), bf16)],
        compiler_params=params(),
        name="bary_pass",
    )(pairs, points_x, points_y, f_pot, g_pot.reshape(col_shape))

    barycenter = pl.pallas_call(
        functools.partial(bary_join_kernel, gy_size),
        out_shape=jax.ShapeDtypeStruct((rows, width), f32),
        in_specs=[VMEM],
        out_specs=VMEM,
        scratch_shapes=[
            pltpu.VMEM((4, width + 8, TILE), f32),
            pltpu.VMEM((3, width + 8, TILE), f32),
            dma((16,)),
            dma((16,)),
        ],
        compiler_params=params(collective_id=2, has_side_effects=True),
        name="bary_join",
    )(partial)
    return (f_pot.reshape(-1), g_pot.reshape(-1), barycenter)


def solution(mesh):
    in_specs = (P("gx", None), P("gy", None), P("gy"), P("gx"), P("gy"), P("gx", None), P("gx"))
    out_specs = (P("gx"), P("gy"), P("gx", None))
    body = functools.partial(local, mesh.shape["gx"], mesh.shape["gy"])
    return jax.shard_map(body, mesh=mesh, in_specs=in_specs, out_specs=out_specs, check_vma=False)
```

time: 965 us -> 99.4 us (0.10); the launches traced: 953 us -> 98 us
  waiting for transfers between devices: 641 us -> 0 us
  loops' own time: 104 us -> 0 us
  Pallas kernels: 0 us -> 89.8 us
  other arithmetic: 85.7 us -> 0 us
  blocking collectives: 43.3 us -> 0 us
  matrix products: 31.1 us -> 0 us
  local copies, waits for them, and re-layouts: 33.2 us -> 7.47 us
  between operations: 14 us -> 0.73 us
    all_gather x2 -> x0, waiting for transfers between devices: 440 us -> none  [merged(): pieces = jax.tree.map(lambda part: lax.all_gather(part, axis), value)]
    psum x1 -> x0, waiting for transfers between devices: 200 us -> none  [local(): total_numer, total_denom = lax.psum((numer, denom.reshape(-1)), 'gy')]
    another operation x5 -> x0, loops' own time: 104 us -> none  [the longest x1 35.7 us: local(): numer, denom = lax.fori_loop(0, live_tiles, bary_step, empty_bary)]
    pallas_call x0 -> x6, Pallas kernels: none -> 89.8 us  [the longest x1 39.4 us: local(): pl.pallas_call(functools.partial(bary_join_kernel, gy_size), out_shape=ja...]
    add x70 -> x0, other arithmetic: 50.6 us -> none  [merge_pair(): left[1] * jnp.exp(left[0] - peak) + right[1] * jnp.exp(right[0] - peak)]
    dot_general x24 -> x0, matrix products: 31.1 us -> none  [the longest x18 23.5 us: tile_pair(): lax.dot_general(x_tile, y_tile, (((1,), (1,)), ((), ())), preferred_eleme...]
    another operation x37 -> x0, other arithmetic: 28.3 us -> none
    all_gather x2 -> x0, blocking collectives: 22.9 us -> none  [merged(): pieces = jax.tree.map(lambda part: lax.all_gather(part, axis), value)]
  transfers between devices with their start and end apart: 3 -> 0, of which waited for: 3 -> 0; matrix products, arithmetic and copies ran while one was open for 0% -> 0% of each run, Pallas kernels for 0% -> 0%
where the time goes in v1:
time: 99.4 us; the launch traced here: 98 us
  Pallas kernels  89.8 us (90%)
  local copies, waits for them, and re-layouts  7.47 us (8%)
    pallas_call x1, Pallas kernels, local(): pl.pallas_call(functools.partial(bary_join_kernel, gy_size), out_shape=ja...  39.4 us
    pallas_call x1, Pallas kernels, local(): pl.pallas_call(functools.partial(col_join_kernel, nz, ny), out_shape=jax....  26.5 us
    pallas_call x1, Pallas kernels, local(): pl.pallas_call(functools.partial(row_join_kernel, gy_size), out_shape=jax...  13.2 us
    unnamed x21, local copies, waits for them, and re-layouts  7.47 us
    pallas_call x1, Pallas kernels, local(): pl.pallas_call(bary_kernel, out_shape=jax.ShapeDtypeStruct((row_tiles, wi...  4.01 us
    pallas_call x1, Pallas kernels, local(): pl.pallas_call(row_kernel, out_shape=(jax.ShapeDtypeStruct(row_shape, f32...  3.75 us
    pallas_call x1, Pallas kernels, local(): pl.pallas_call(column_kernel, out_shape=jax.ShapeDtypeStruct(col_shape, f...  2.93 us

profile of v1, /device:TPU:1, one launch (start us, length us, event | category | flops | bytes accessed | tf_op | source)
XLA Modules:
  0.0 98.0 jit_solution(13657463904660419555)
XLA Ops:
  0.6 0.0 copy-start
  0.6 1.6 %copy-done = bf16[8192,128]{1,0:T(8,128)(2,1)S(1)} copy-done((bf16[8192,128]{1,0:T(8,128)(2,1)S(1)}, bf16[8192,128]{1,0:T(8,128)(2,1)}, u32[]{:S(2)}) %copy-start) | copy-done | bytes 2097176
  2.2 0.0 copy-start.2
  2.2 1.2 %copy-done.2 = bf16[4096,128]{1,0:T(8,128)(2,1)S(1)} copy-done((bf16[4096,128]{1,0:T(8,128)(2,1)S(1)}, bf16[4096,128]{1,0:T(8,128)(2,1)}, u32[]{:S(2)}) %copy-start.2) | copy-done | bytes 1048600
  3.4 0.0 copy-start.4
  3.5 0.8 copy-done.4
  4.2 0.0 copy-start.7
  4.2 0.7 copy-done.7
  4.9 0.0 copy-start.8
  4.9 0.7 copy-done.8
  5.6 3.8 %row_pass.1 = (f32[32,128]{1,0:T(8,128)S(1)}, s32[129]{0:T(256)S(1)}) custom-call(s32[8,16]{1,0:T(8,128)S(1)} %copy-done.7, s32[8]{0:T(128)S(1)} %copy-done.8, bf16[4096,128]{1,0:T(8,128)(2,1)S(1)} %copy-done.2, bf16[8192,128]{1,0:T(8,128)(2,1)S(1)} %copy-done, f32[64,128]{1,0:T(8,128)S(1)} %bitcast.11), custom_call_target="tpu_custom_call" | custom-call | tf_op jit(solution)/shard_map/row_pass/pallas_call | solution.py:312
  9.3 0.0 copy-start.5
  9.3 0.0 copy-done.6
  9.3 13.2 %row_join.1.f_ref = f32[32,128]{1,0:T(8,128)S(1)} custom-call(f32[32,128]{1,0:T(8,128)S(1)} %get-tuple-element.5.lse_ref, f32[32,128]{1,0:T(8,128)S(1)} %bitcast.13), custom_call_target="tpu_custom_call" | custom-call | tf_op jit(solution)/shard_map/row_join/pallas_call | solution.py:325
  22.5 0.0 copy-done.1
  22.5 0.0 copy-done.3
  22.5 2.9 %column_pass.1 = f32[64,128]{1,0:T(8,128)S(1)} custom-call(s32[129]{0:T(256)S(1)} %get-tuple-element.6.list_ref, bf16[4096,128]{1,0:T(8,128)(2,1)S(1)} %copy-done.3, bf16[8192,128]{1,0:T(8,128)(2,1)S(1)} %copy-done.1, f32[32,128]{1,0:T(8,128)S(1)} %row_join.1.f_ref), custom_call_target="tpu_custom_call" | custom-call | tf_op jit(solution)/shard_map/column_pass/pallas_call | solution.py:339
  25.5 0.0 copy-done.5
  25.5 26.5 %column_join.1 = f32[8,8,128]{2,1,0:T(8,128)S(1)} custom-call(f32[8,8,128]{2,1,0:T(8,128)S(1)} %bitcast.10, f32[8,8,128]{2,1,0:T(8,128)S(1)} %bitcast.12), custom_call_target="tpu_custom_call" | custom-call | tf_op jit(solution)/shard_map/column_join/pallas_call | solution.py:350
  52.0 4.0 %bary_pass.1.part_ref = f32[8,136,512]{2,1,0:T(8,128)S(1)} custom-call(s32[129]{0:T(256)S(1)} %get-tuple-element.6.list_ref, bf16[4096,128]{1,0:T(8,128)(2,1)S(1)} %copy-done.3, bf16[8192,128]{1,0:T(8,128)(2,1)S(1)} %copy-done.1, f32[32,128]{1,0:T(8,128)S(1)} %row_join.1.f_ref, f32[64,128]{1,0:T(8,128)S(1)} %bitcast.7), custom_call_target="tpu_custom_call" | custom-call | tf_op jit(solution)/shard_map/bary_pass/pallas_call | solution.py:366
  56.0 39.4 %bary_join.1 = f32[4096,128]{1,0:T(8,128)S(1)} custom-call(f32[8,136,512]{2,1,0:T(8,128)S(1)} %bary_pass.1.part_ref), custom_call_target="tpu_custom_call" | custom-call | tf_op jit(solution)/shard_map/bary_join/pallas_call | solution.py:376
  95.5 0.6 copy.13
  96.1 0.6 copy.14
  96.7 1.3 %copy.15 = f32[4096,128]{1,0:T(8,128)} copy(f32[4096,128]{1,0:T(8,128)S(1)} %bary_join.1) | data formatting | bytes 4194304
  (3 shorter events, 0.0 us)
Async XLA Ops:
  0.6 1.6 %copy-start = (bf16[8192,128]{1,0:T(8,128)(2,1)S(1)}, bf16[8192,128]{1,0:T(8,128)(2,1)}, u32[]{:S(2)}) copy-start(bf16[8192,128]{1,0:T(8,128)(2,1)} %y_ref.5) | copy-start | bytes 6291460
  2.2 1.2 %copy-start.2 = (bf16[4096,128]{1,0:T(8,128)(2,1)S(1)}, bf16[4096,128]{1,0:T(8,128)(2,1)}, u32[]{:S(2)}) copy-start(bf16[4096,128]{1,0:T(8,128)(2,1)} %x_ref.5) | copy-start | bytes 3145732
  3.4 0.8 copy-start.4
  4.2 0.7 copy-start.7
  4.9 0.7 copy-start.8
  5.6 3.8 %copy-start.6 = (f32[4096]{0:T(1024)S(1)}, f32[4096]{0:T(1024)}, u32[]{:S(2)}) copy-start(f32[4096]{0:T(1024)} %param.10) | copy-start | bytes 49156
  5.6 16.9 %copy-start.1 = (bf16[8192,128]{1,0:T(8,128)(2,1)S(1)}, bf16[8192,128]{1,0:T(8,128)(2,1)}, u32[]{:S(2)}) copy-start(bf16[8192,128]{1,0:T(8,128)(2,1)} %y_ref.5) | copy-start | bytes 6291460
  5.6 17.0 %copy-start.3 = (bf16[4096,128]{1,0:T(8,128)(2,1)S(1)}, bf16[4096,128]{1,0:T(8,128)(2,1)}, u32[]{:S(2)}) copy-start(bf16[4096,128]{1,0:T(8,128)(2,1)} %x_ref.5) | copy-start | bytes 3145732
  9.3 16.1 %copy-start.5 = (f32[8192]{0:T(1024)S(1)}, f32[8192]{0:T(1024)}, u32[]{:S(2)}) copy-start(f32[8192]{0:T(1024)} %param.11) | copy-start | bytes 98308

commit v2 on v1

v2 whole, which is shorter than its diff:
```python
import functools

import jax
import jax.numpy as jnp
from jax import lax
from jax.experimental import pallas as pl
from jax.experimental.pallas import tpu as pltpu
from jax.sharding import PartitionSpec as P

TILE = 512
LANES = 128
CHUNKS = TILE // LANES
LSE_GROUP = 2
BARY_GROUP = 3
PIECES = 2
MESH = pl.DeviceIdType.MESH
NEG_FILL = -1e30
SCALE = 2.8853900817779268
VMEM = pl.BlockSpec(memory_space=pltpu.VMEM)
SMEM = pl.BlockSpec(memory_space=pltpu.SMEM)
HBM = pl.BlockSpec(memory_space=pltpu.HBM)
VMEM_LIMIT = 40 * 1024 * 1024


def params(**kw):
    return pltpu.CompilerParams(vmem_limit_bytes=VMEM_LIMIT, **kw)


def split3(value):
    high = value.astype(jnp.bfloat16).astype(jnp.float32)
    rest = value - high
    middle = rest.astype(jnp.bfloat16).astype(jnp.float32)
    low = (rest - middle).astype(jnp.bfloat16).astype(jnp.float32)
    return [high, middle, low]


def tile_rows(ref, tiles):
    return jnp.concatenate(
        [ref[pl.ds(q, tiles, stride=CHUNKS), :] for q in range(CHUNKS)], axis=1
    )


def as_columns(pieces):
    rows = sum(piece.shape[0] for piece in pieces)
    pieces = pieces + [jnp.zeros((LANES - rows, TILE), jnp.float32)]
    return jnp.concatenate(pieces, axis=0).T.astype(jnp.bfloat16)


def lane_mask(first, period, which):
    lane = lax.broadcasted_iota(jnp.int32, (1, LANES), 1) - first
    hit = (lane == which) | (lane == which + period) | (lane == which + 2 * period)
    return jnp.where(hit, 1.0, 0.0)


def spread(row):
    return jnp.broadcast_to(row, (TILE, LANES)).astype(jnp.bfloat16)


def tile_at(ref, index):
    return ref[pl.ds(pl.multiple_of(index * TILE, TILE), TILE), :]


def product(left, right):
    return lax.dot_general(
        left, right, (((1,), (1,)), ((), ())), preferred_element_type=jnp.float32
    )


def pair_at(list_ref, live, at):
    return list_ref[jnp.minimum(at, live - 1)]


def pipelined(size, live, fill, drain, add=None):
    groups = lax.div(live + (size - 1), size)

    def step(group, carry):
        if add is not None:
            add(group - 1)
        drain(group)
        fill(group + 1)
        return carry

    if add is None:

        @pl.when(groups > 0)
        def _():
            fill(0)
            lax.fori_loop(0, groups - 1, step, 0)
            drain(groups - 1)

        return

    @pl.when(groups > 1)
    def _():
        fill(0)
        drain(0)
        fill(1)
        lax.fori_loop(1, groups - 1, step, 0)
        add(groups - 2)
        drain(groups - 1)
        add(groups - 1)

    @pl.when(groups == 1)
    def _():
        fill(0)
        drain(0)
        add(0)


def fold_rows(value, op):
    rows, lanes = value.shape
    return op(op(value.reshape(4, rows // 32, 8, lanes), axis=1), axis=0)


def lse_pass(
    list_ref, live, pick, outer_ref, inner_ref, pot_tiles, columns, peak, mass, sums, tops
):
    peak[...] = jnp.full_like(peak, NEG_FILL)
    mass[...] = jnp.zeros_like(mass)
    spare = peak.shape[0] - 1

    def fill(group):
        for u in range(LSE_GROUP):
            outer, inner = pick(pair_at(list_ref, live, group * LSE_GROUP + u))
            left = jnp.concatenate([tile_at(outer_ref, outer), columns[...]], axis=1)
            right = jnp.concatenate(
                [tile_at(inner_ref, inner), spread(lane_mask(0, pot_tiles, outer))], axis=1
            )
            value = product(left, right)
            sums[u] = value
            tops[u] = fold_rows(value, jnp.max)

    def drain(group):
        for u in range(LSE_GROUP):
            at = group * LSE_GROUP + u
            inner = jnp.where(at < live, pick(pair_at(list_ref, live, at))[1], spare)
            before = peak[inner]
            top = jnp.maximum(before, tops[u])
            value = sums[u].reshape(TILE // 8, 8, TILE) - top[None]
            terms = fold_rows(jnp.exp2(value * SCALE).reshape(TILE, TILE), jnp.sum)
            mass[inner] = mass[inner] * jnp.exp2((before - top) * SCALE) + terms
            peak[inner] = top

    pipelined(LSE_GROUP, live, fill, drain)


def lse_finish(peak, mass, out_ref):
    for tile in range(peak.shape[0] - 1):
        top = jnp.max(peak[tile], axis=0, keepdims=True)
        total = jnp.sum(mass[tile] * jnp.exp2((peak[tile] - top) * SCALE), axis=0, keepdims=True)
        lse = jnp.where(total > 0.0, 2.0 * top + jnp.log(total), NEG_FILL)
        for q in range(CHUNKS):
            out_ref[pl.ds(tile * CHUNKS + q, 1), :] = lse[:, q * LANES : (q + 1) * LANES]


def list_kernel(col_tiles, cols_ref, counts_ref, list_ref):
    row_tiles, most = cols_ref.shape
    me = lax.axis_index("gy")
    live = jnp.int32(0)
    for row in range(row_tiles):
        count = counts_ref[row]
        for slot in range(most):
            at = cols_ref[row, slot] - me * col_tiles
            owned = (at >= 0) & (at < col_tiles) & (slot < count)
            list_ref[live] = row * col_tiles + at
            live = live + jnp.where(owned, 1, 0)
    list_ref[row_tiles * most] = live


def row_kernel(list_ref, x_ref, y_ref, g_ref, lse_ref, columns, *sums):
    col_tiles = y_ref.shape[0] // TILE
    live = list_ref[list_ref.shape[0] - 1]
    columns[...] = as_columns(split3(tile_rows(g_ref, col_tiles)))
    pick = lambda pair: (lax.rem(pair, col_tiles), lax.div(pair, col_tiles))
    lse_pass(list_ref, live, pick, y_ref, x_ref, col_tiles, columns, *sums)
    lse_finish(*sums[:2], lse_ref)


def column_kernel(list_ref, x_ref, y_ref, f_ref, lse_ref, columns, *sums):
    row_tiles = x_ref.shape[0] // TILE
    col_tiles = y_ref.shape[0] // TILE
    live = list_ref[list_ref.shape[0] - 1]
    columns[...] = as_columns(split3(tile_rows(f_ref, row_tiles)))
    pick = lambda pair: (lax.div(pair, col_tiles), lax.rem(pair, col_tiles))
    lse_pass(list_ref, live, pick, x_ref, y_ref, row_tiles, columns, *sums)
    lse_finish(*sums[:2], lse_ref)


def bary_kernel(
    list_ref,
    x_ref,
    y_ref,
    f_ref,
    g_ref,
    out_ref,
    f_hbm,
    g_hbm,
    columns,
    pots_g,
    pots_f,
    sums,
    rounded,
    sems,
):
    results = [
        pltpu.make_async_copy(f_ref, f_hbm, sems.at[0]),
        pltpu.make_async_copy(g_ref, g_hbm, sems.at[1]),
    ]
    for copy in results:
        copy.start()
    row_tiles = x_ref.shape[0] // TILE
    col_tiles = y_ref.shape[0] // TILE
    width = x_ref.shape[1]
    live = list_ref[list_ref.shape[0] - 1]
    first = 3 * col_tiles
    pots = split3(tile_rows(g_ref, col_tiles)) + split3(tile_rows(f_ref, row_tiles))
    columns[...] = as_columns(pots)
    out_ref[...] = jnp.zeros_like(out_ref)

    spare = out_ref.shape[0] - 1
    lane = lax.broadcasted_iota(jnp.int32, (1, LANES), 1)
    of_g = spread(jnp.where(lane < first, 1.0, 0.0))
    of_f = spread(jnp.where(lane < first, 0.0, 1.0))
    pots_g[...] = columns[...] * of_g
    pots_f[...] = columns[...] * of_f
    pick = lambda pair: (lax.div(pair, col_tiles), lax.rem(pair, col_tiles))

    def fill(group):
        for u in range(BARY_GROUP):
            row, col = pick(pair_at(list_ref, live, group * BARY_GROUP + u))
            left = jnp.concatenate(
                [tile_at(y_ref, col), pots_g[...] + spread(lane_mask(first, row_tiles, row))],
                axis=1,
            )
            right = jnp.concatenate(
                [tile_at(x_ref, row), pots_f[...] + spread(lane_mask(0, col_tiles, col))], axis=1
            )
            sums[u] = product(left, right)

    def drain(group):
        for u in range(BARY_GROUP):
            at = group * BARY_GROUP + u
            row = jnp.where(at < live, pick(pair_at(list_ref, live, at))[0], spare)
            weights = jnp.exp2(sums[u] * SCALE)
            out_ref[row, width:] += fold_rows(weights, jnp.sum)
            rounded[u] = weights.astype(jnp.bfloat16)

    def add(group):
        for u in range(BARY_GROUP):
            at = group * BARY_GROUP + u
            row, col = pick(pair_at(list_ref, live, at))
            row = jnp.where(at < live, row, spare)
            out_ref[row, :width] += lax.dot_general(
                tile_at(y_ref, col),
                rounded[u],
                (((0,), (0,)), ((), ())),
                preferred_element_type=jnp.float32,
            )

    pipelined(BARY_GROUP, live, fill, drain, add)
    for copy in results:
        copy.wait()


def meet(peers):
    barrier = pltpu.get_barrier_semaphore()
    for peer in peers:
        pl.semaphore_signal(barrier, inc=1, device_id=peer, device_id_type=MESH)
    pl.semaphore_wait(barrier, len(peers))


def send(src, dst, send_sem, recv_sem, peer):
    copy = pltpu.make_async_remote_copy(
        src_ref=src,
        dst_ref=dst,
        send_sem=send_sem,
        recv_sem=recv_sem,
        device_id=peer,
        device_id_type=MESH,
    )
    copy.start()
    return copy


def join(parts):
    top = parts[0]
    for part in parts[1:]:
        top = jnp.maximum(top, part)
    total = jnp.exp(parts[0] - top)
    for part in parts[1:]:
        total = total + jnp.exp(part - top)
    return top + jnp.log(total)


def row_join_kernel(n, lse_ref, log_a_ref, f_ref, held, send_sem, recv_sem):
    me = lax.axis_index("gy")
    peers = [{"gy": lax.rem(me + d, n)} for d in range(1, n)]
    meet(peers)
    copies = [
        send(lse_ref, held.at[me], send_sem.at[i], recv_sem.at[i], peer)
        for i, peer in enumerate(peers)
    ]
    held[me] = lse_ref[...]
    for copy in copies:
        copy.wait()
    f_ref[...] = 0.5 * (log_a_ref[...] - join([held[k] for k in range(n)]))


def col_join_kernel(nz, ny, lse_ref, log_b_ref, g_ref, first, part, second, sems):
    me = lax.axis_index("gx")
    z, y = lax.div(me, ny), lax.rem(me, ny)
    y_peers = [{"gx": z * ny + lax.rem(y + d, ny)} for d in range(1, ny)]
    z_peers = [{"gx": lax.rem(z + d, nz) * ny + y} for d in range(1, nz)]
    meet(y_peers + z_peers)
    half = lse_ref.shape[0] // 2
    n = ny
    for stage in range(2):
        held = (first, second)[stage]
        copies = []
        for upper in range(2):
            own = lse_ref.at[pl.ds(upper * half, half)] if stage == 0 else part.at[upper]
            along_y = upper == stage
            at = y if along_y else z
            for i, peer in enumerate(y_peers if along_y else z_peers):
                k = (stage * 2 + upper) * (n - 1) + i
                copies.append(send(own, held.at[upper, at], sems.at[0, k], sems.at[1, k], peer))
            held[upper, at] = own[...]
        for copy in copies:
            copy.wait()
        for upper in range(2):
            joined = join([held[upper, k] for k in range(n)])
            if stage == 0:
                part[upper] = joined
            else:
                rows = slice(upper * half, (upper + 1) * half)
                g_ref[rows] = 0.5 * (log_b_ref[rows] - joined)


def bary_join_kernel(n, part_ref, out_ref, near, relay, left_in, right_in, sems):
    me = lax.axis_index("gy")
    chips = n // 2
    chip, core = lax.div(me, 2), lax.rem(me, 2)
    other = 1 - core
    width = out_ref.shape[1]
    split = width // 2
    low, high = slice(0, split), slice(split, width + 8)
    places = [lax.rem(chip + d, chips) for d in range(chips)]
    sibling = {"gy": chip * 2 + other}
    right, left = {"gy": places[1] * 2 + core}, {"gy": places[3] * 2 + core}
    meet([sibling, right, left])
    used = [0]

    def go(src, dst, peer):
        k = used[0]
        used[0] += 1
        return send(src, dst, sems.at[0, k], sems.at[1, k], peer)

    pieces = [slice(k * TILE // PIECES, (k + 1) * TILE // PIECES) for k in range(PIECES)]
    inside = {d: go(part_ref.at[places[d] * 2 + other], near.at[d], sibling) for d in (2, 1, 3, 0)}
    waits = []

    def add_inside(d):
        inside[d].wait()
        near[d] = near[d] + part_ref[places[d] * 2 + core]

    add_inside(2)
    far = []
    for piece in pieces:
        far.append(
            (
                go(near.at[2, low, piece], relay.at[low, piece], right),
                go(near.at[2, high, piece], relay.at[high, piece], left),
            )
        )
    add_inside(1)
    add_inside(3)
    direct, passed = [], []
    for k, piece in enumerate(pieces):
        direct.append(
            (
                go(near.at[1, high, piece], left_in.at[high, piece], right),
                go(near.at[3, low, piece], right_in.at[low, piece], left),
            )
        )
        if k == 0:
            add_inside(0)
        far[k][0].wait()
        near[1, low, piece] = near[1, low, piece] + relay[low, piece]
        to_right = go(near.at[1, low, piece], left_in.at[low, piece], right)
        far[k][1].wait()
        near[3, high, piece] = near[3, high, piece] + relay[high, piece]
        to_left = go(near.at[3, high, piece], right_in.at[high, piece], left)
        passed.append((to_right, to_left))

    def rows_of(place, kind, first, count):
        start = (place * 2 + kind) * TILE + first
        return out_ref.at[pl.ds(pl.multiple_of(start, 8), count)]

    size = TILE // PIECES
    own = []
    for k, piece in enumerate(pieces):
        for copy in direct[k] + passed[k]:
            copy.wait()
        total = near[0, :, piece] + left_in[:, piece] + right_in[:, piece]
        ratio = total[:width] / jnp.sum(total[width:], axis=0, keepdims=True)
        mine = rows_of(chip, core, k * size, size)
        mine[...] = ratio.T
        own.append((go(mine, mine, right), go(mine, mine, left)))
        waits.append(go(mine, mine, sibling))
    onward = []
    for k in range(PIECES):
        for side in range(2):
            own[k][side].wait()
            place = places[3] if side == 0 else places[1]
            block = rows_of(place, core, k * size + side * size // 2, size // 2)
            onward.append((k, side, go(block, block, right if side == 0 else left)))
            block = rows_of(place, core, k * size, size)
            waits.append(go(block, block, sibling))
    for k, side, copy in onward:
        copy.wait()
        block = rows_of(places[2], core, k * size + side * size // 2, size // 2)
        waits.append(go(block, block, sibling))
    for copy in waits:
        copy.wait()


def local(gx_size, gy_size, points_x, points_y, g_init, log_a, log_b, tile_cols, tile_counts):
    row_tiles, most = tile_cols.shape
    rows, width = points_x.shape
    cols = points_y.shape[0]
    col_tiles = cols // TILE
    nz = 1
    while nz * nz < gx_size:
        nz *= 2
    ny = gx_size // nz
    f32, i32, bf16 = jnp.float32, jnp.int32, jnp.bfloat16
    row_shape, col_shape = (rows // LANES, LANES), (cols // LANES, LANES)
    dma = pltpu.SemaphoreType.DMA

    def lse_scratch(tiles):
        return [
            pltpu.VMEM((TILE, LANES), bf16),
            pltpu.VMEM((tiles + 1, 8, TILE), f32),
            pltpu.VMEM((tiles + 1, 8, TILE), f32),
            pltpu.VMEM((LSE_GROUP, TILE, TILE), f32),
            pltpu.VMEM((LSE_GROUP, 8, TILE), f32),
        ]

    pairs = pl.pallas_call(
        functools.partial(list_kernel, col_tiles),
        out_shape=jax.ShapeDtypeStruct((row_tiles * most + 1,), i32),
        in_specs=[SMEM, SMEM],
        out_specs=SMEM,
        compiler_params=params(),
        name="list_pairs",
    )(tile_cols, tile_counts)

    row_lse = pl.pallas_call(
        row_kernel,
        out_shape=jax.ShapeDtypeStruct(row_shape, f32),
        in_specs=[SMEM, VMEM, VMEM, VMEM],
        out_specs=VMEM,
        scratch_shapes=lse_scratch(row_tiles),
        compiler_params=params(),
        name="row_pass",
    )(pairs, points_x, points_y, g_init.reshape(col_shape))

    f_pot = pl.pallas_call(
        functools.partial(row_join_kernel, gy_size),
        out_shape=jax.ShapeDtypeStruct(row_shape, f32),
        in_specs=[VMEM, VMEM],
        out_specs=VMEM,
        scratch_shapes=[
            pltpu.VMEM((gy_size,) + row_shape, f32),
            dma((gy_size - 1,)),
            dma((gy_size - 1,)),
        ],
        compiler_params=params(collective_id=0, has_side_effects=True),
        name="row_join",
    )(row_lse, log_a.reshape(row_shape))

    col_lse = pl.pallas_call(
        column_kernel,
        out_shape=jax.ShapeDtypeStruct(col_shape, f32),
        in_specs=[SMEM, VMEM, VMEM, VMEM],
        out_specs=VMEM,
        scratch_shapes=lse_scratch(col_tiles),
        compiler_params=params(),
        name="column_pass",
    )(pairs, points_x, points_y, f_pot)

    half = (2, col_shape[0] // 2, LANES)
    g_pot = pl.pallas_call(
        functools.partial(col_join_kernel, nz, ny),
        out_shape=jax.ShapeDtypeStruct(col_shape, f32),
        in_specs=[VMEM, VMEM],
        out_specs=VMEM,
        scratch_shapes=[
            pltpu.VMEM((2, ny) + half[1:], f32),
            pltpu.VMEM(half, f32),
            pltpu.VMEM((2, ny) + half[1:], f32),
            dma((2, 4 * (ny - 1))),
        ],
        compiler_params=params(collective_id=1, has_side_effects=True),
        name="column_join",
    )(col_lse, log_b.reshape(col_shape))

    partial, f_pot, g_pot = pl.pallas_call(
        bary_kernel,
        out_shape=(
            jax.ShapeDtypeStruct((row_tiles + 1, width + 8, TILE), f32),
            jax.ShapeDtypeStruct(row_shape, f32),
            jax.ShapeDtypeStruct(col_shape, f32),
        ),
        in_specs=[SMEM, VMEM, VMEM, VMEM, VMEM],
        out_specs=(VMEM, HBM, HBM),
        scratch_shapes=[pltpu.VMEM((TILE, LANES), bf16)] * 3
        + [
            pltpu.VMEM((BARY_GROUP, TILE, TILE), f32),
            pltpu.VMEM((BARY_GROUP, TILE, TILE), bf16),
            dma((2,)),
        ],
        compiler_params=params(),
        name="bary_pass",
    )(pairs, points_x, points_y, f_pot, g_pot)

    barycenter = pl.pallas_call(
        functools.partial(bary_join_kernel, gy_size),
        out_shape=jax.ShapeDtypeStruct((rows, width), f32),
        in_specs=[VMEM],
        out_specs=VMEM,
        scratch_shapes=[pltpu.VMEM((4, width + 8, TILE), f32)]
        + [pltpu.VMEM((width + 8, TILE), f32)] * 3
        + [dma((2, 4 + 15 * PIECES))],
        compiler_params=params(collective_id=2, has_side_effects=True),
        name="bary_join",
    )(partial)
    return (f_pot.reshape(-1), g_pot.reshape(-1), barycenter)


def solution(mesh):
    in_specs = (P("gx", None), P("gy", None), P("gy"), P("gx"), P("gy"), P("gx", None), P("gx"))
    out_specs = (P("gx"), P("gy"), P("gx", None))
    body = functools.partial(local, mesh.shape["gx"], mesh.shape["gy"])
    return jax.shard_map(body, mesh=mesh, in_specs=in_specs, out_specs=out_specs, check_vma=False)
```

time: 99.4 us -> 80.3 us (0.81)
  Pallas kernels: 89.8 us -> 72.9 us
  local copies, waits for them, and re-layouts: 7.47 us -> 6.24 us
    pallas_call x1, Pallas kernels: 39.4 us -> 29.1 us  [local(): pl.pallas_call(functools.partial(bary_join_kernel, gy_size), out_shape=ja...]
    pallas_call x1, Pallas kernels: 26.5 us -> 20.2 us  [local(): pl.pallas_call(functools.partial(col_join_kernel, nz, ny), out_shape=jax....]
    unnamed x21 -> x17, local copies, waits for them, and re-layouts: 7.47 us -> 6.24 us
    pallas_call x2 -> x3, Pallas kernels: 7.76 us -> 7.12 us  [the longest x1 2.85 us: local(): pl.pallas_call(bary_kernel, out_shape=(jax.ShapeDtypeStruct((row_tiles +...]
where the time goes in v2:
time: 80.3 us; the launch traced here: 79.9 us
  Pallas kernels  72.9 us (91%)
  local copies, waits for them, and re-layouts  6.24 us (8%)
    pallas_call x1, Pallas kernels, local(): pl.pallas_call(functools.partial(bary_join_kernel, gy_size), out_shape=ja...  29.1 us
    pallas_call x1, Pallas kernels, local(): pl.pallas_call(functools.partial(col_join_kernel, nz, ny), out_shape=jax....  20.2 us
    pallas_call x1, Pallas kernels, local(): pl.pallas_call(functools.partial(row_join_kernel, gy_size), out_shape=jax...  13.8 us
    unnamed x17, local copies, waits for them, and re-layouts  6.24 us
    pallas_call x1, Pallas kernels, local(): pl.pallas_call(bary_kernel, out_shape=(jax.ShapeDtypeStruct((row_tiles +...  2.85 us
    pallas_call x1, Pallas kernels, local(): pl.pallas_call(column_kernel, out_shape=jax.ShapeDtypeStruct(col_shape, f...  2.69 us
    pallas_call x1, Pallas kernels, local(): pl.pallas_call(row_kernel, out_shape=jax.ShapeDtypeStruct(row_shape, f32)...  2.59 us
    pallas_call x1, Pallas kernels, local(): pl.pallas_call(functools.partial(list_kernel, col_tiles), out_shape=jax.S...  1.68 us

profile of v2, /device:TPU:1, one launch (start us, length us, event | category | flops | bytes accessed | tf_op | source)
XLA Modules:
  0.0 79.9 jit_solution(12785763796446803568)
XLA Ops:
  0.6 0.0 copy-start.6
  0.6 0.7 copy-done.6
  1.3 0.0 copy-start.7
  1.3 0.7 copy-done.7
  2.0 1.7 %list_pairs.1.list_ref = s32[129]{0:T(256)S(1)} custom-call(s32[8,16]{1,0:T(8,128)S(1)} %copy-done.6, s32[8]{0:T(128)S(1)} %copy-done.7), custom_call_target="tpu_custom_call" | custom-call | tf_op jit(solution)/shard_map/list_pairs/pallas_call | solution.py:449
  3.7 0.0 copy-start
  3.7 1.6 %copy-done = bf16[8192,128]{1,0:T(8,128)(2,1)S(1)} copy-done((bf16[8192,128]{1,0:T(8,128)(2,1)S(1)}, bf16[8192,128]{1,0:T(8,128)(2,1)}, u32[]{:S(2)}) %copy-start) | copy-done | bytes 2097176
  5.3 0.0 copy-start.1
  5.3 1.2 %copy-done.1 = bf16[4096,128]{1,0:T(8,128)(2,1)S(1)} copy-done((bf16[4096,128]{1,0:T(8,128)(2,1)S(1)}, bf16[4096,128]{1,0:T(8,128)(2,1)}, u32[]{:S(2)}) %copy-start.1) | copy-done | bytes 1048600
  6.5 0.0 copy-start.3
  6.5 0.8 copy-done.3
  7.2 0.0 copy-start.5
  7.2 0.0 copy-start.2
  7.2 2.6 %row_pass.1.lse_ref = f32[32,128]{1,0:T(8,128)S(1)} custom-call(s32[129]{0:T(256)S(1)} %list_pairs.1.list_ref, bf16[4096,128]{1,0:T(8,128)(2,1)S(1)} %copy-done.1, bf16[8192,128]{1,0:T(8,128)(2,1)S(1)} %copy-done, f32[64,128]{1,0:T(8,128)S(1)} %bitcast.5), custom_call_target="tpu_custom_call" | custom-call | tf_op jit(solution)/shard_map/row_pass/pallas_call | solution.py:458
  9.8 0.0 copy-done.5
  9.8 0.0 copy-start.4
  9.9 13.8 %row_join.1.f_ref = f32[32,128]{1,0:T(8,128)S(1)} custom-call(f32[32,128]{1,0:T(8,128)S(1)} %row_pass.1.lse_ref, f32[32,128]{1,0:T(8,128)S(1)} %bitcast.7), custom_call_target="tpu_custom_call" | custom-call | tf_op jit(solution)/shard_map/row_join/pallas_call | solution.py:468
  23.7 0.0 copy-done.2
  23.7 2.7 %column_pass.1.lse_ref = f32[64,128]{1,0:T(8,128)S(1)} custom-call(s32[129]{0:T(256)S(1)} %list_pairs.1.list_ref, bf16[4096,128]{1,0:T(8,128)(2,1)S(1)} %copy-done.2, bf16[8192,128]{1,0:T(8,128)(2,1)S(1)} %copy-done, f32[32,128]{1,0:T(8,128)S(1)} %row_join.1.f_ref), custom_call_target="tpu_custom_call" | custom-call | tf_op jit(solution)/shard_map/column_pass/pallas_call | solution.py:482
  26.4 0.0 copy-done.4
  26.4 20.2 %column_join.1.g_ref = f32[64,128]{1,0:T(8,128)S(1)} custom-call(f32[64,128]{1,0:T(8,128)S(1)} %column_pass.1.lse_ref, f32[64,128]{1,0:T(8,128)S(1)} %bitcast.6), custom_call_target="tpu_custom_call" | custom-call | tf_op jit(solution)/shard_map/column_join/pallas_call | solution.py:493
  46.6 2.9 %bary_pass.1 = (f32[9,136,512]{2,1,0:T(8,128)S(1)}, f32[32,128]{1,0:T(8,128)}, f32[64,128]{1,0:T(8,128)}) custom-call(s32[129]{0:T(256)S(1)} %list_pairs.1.list_ref, bf16[4096,128]{1,0:T(8,128)(2,1)S(1)} %copy-done.2, bf16[8192,128]{1,0:T(8,128)(2,1)S(1)} %copy-done, f32[32,128]{1,0:T(8,128)S(1)} %row_join.1.f_ref, f32[64,128]{1,0:T(8,128)S(1)} %column_join.1.g_ref), custom_call_target="tpu_custom_call" | custom-call | tf_op jit(solution)/shard_map/bary_pass/pallas_call | solution.py:508
  49.4 29.1 %bary_join.1 = f32[4096,128]{1,0:T(8,128)S(1)} custom-call(f32[9,136,512]{2,1,0:T(8,128)S(1)} %get-tuple-element.8.part_ref), custom_call_target="tpu_custom_call" | custom-call | tf_op jit(solution)/shard_map/bary_join/pallas_call | solution.py:527
  78.6 1.3 %copy.11 = f32[4096,128]{1,0:T(8,128)} copy(f32[4096,128]{1,0:T(8,128)S(1)} %bary_join.1) | data formatting | bytes 4194304
Async XLA Ops:
  0.6 0.7 copy-start.6
  1.3 0.7 copy-start.7
  3.7 1.6 %copy-start = (bf16[8192,128]{1,0:T(8,128)(2,1)S(1)}, bf16[8192,128]{1,0:T(8,128)(2,1)}, u32[]{:S(2)}) copy-start(bf16[8192,128]{1,0:T(8,128)(2,1)} %y_ref.5) | copy-start | bytes 6291460
  5.3 1.2 %copy-start.1 = (bf16[4096,128]{1,0:T(8,128)(2,1)S(1)}, bf16[4096,128]{1,0:T(8,128)(2,1)}, u32[]{:S(2)}) copy-start(bf16[4096,128]{1,0:T(8,128)(2,1)} %x_ref.5) | copy-start | bytes 3145732
  6.5 0.8 copy-start.3
  7.2 2.6 %copy-start.5 = (f32[4096]{0:T(1024)S(1)}, f32[4096]{0:T(1024)}, u32[]{:S(2)}) copy-start(f32[4096]{0:T(1024)} %param.10) | copy-start | bytes 49156
  7.2 16.4 %copy-start.2 = (bf16[4096,128]{1,0:T(8,128)(2,1)S(1)}, bf16[4096,128]{1,0:T(8,128)(2,1)}, u32[]{:S(2)}) copy-start(bf16[4096,128]{1,0:T(8,128)(2,1)} %x_ref.5) | copy-start | bytes 3145732
  9.8 16.5 %copy-start.4 = (f32[8192]{0:T(1024)S(1)}, f32[8192]{0:T(1024)}, u32[]{:S(2)}) copy-start(f32[8192]{0:T(1024)} %param.11) | copy-start | bytes 98308

commit v3 on v2

--- a/solution.py
+++ b/solution.py
@@ -12,7 +12,7 @@
 CHUNKS = TILE // LANES
 LSE_GROUP = 2
 BARY_GROUP = 3
-PIECES = 2
+PIECES = 4
 MESH = pl.DeviceIdType.MESH
 NEG_FILL = -1e30
 SCALE = 2.8853900817779268
@@ -153,24 +153,48 @@
             out_ref[pl.ds(tile * CHUNKS + q, 1), :] = lse[:, q * LANES : (q + 1) * LANES]
 
 
-def list_kernel(col_tiles, cols_ref, counts_ref, list_ref):
+def row_kernel(
+    cols_hbm,
+    counts_hbm,
+    g_hbm,
+    y_hbm,
+    x_hbm,
+    lse_ref,
+    list_ref,
+    x_ref,
+    y_ref,
+    cols_ref,
+    counts_ref,
+    g_ref,
+    sems,
+    columns,
+    *sums,
+):
+    arrivals = [(cols_hbm, cols_ref), (counts_hbm, counts_ref), (g_hbm, g_ref)]
+    arrivals += [(y_hbm, y_ref), (x_hbm, x_ref)]
+    copies = [
+        pltpu.make_async_copy(src, dst, sems.at[i]) for i, (src, dst) in enumerate(arrivals)
+    ]
+    for copy in copies:
+        copy.start()
     row_tiles, most = cols_ref.shape
+    col_tiles = y_ref.shape[0] // TILE
     me = lax.axis_index("gy")
+    for copy in copies[:3]:
+        copy.wait()
+    columns[...] = as_columns(split3(tile_rows(g_ref, col_tiles)))
     live = jnp.int32(0)
     for row in range(row_tiles):
         count = counts_ref[row]
+        base = (row - me) * col_tiles
         for slot in range(most):
-            at = cols_ref[row, slot] - me * col_tiles
-            owned = (at >= 0) & (at < col_tiles) & (slot < count)
-            list_ref[live] = row * col_tiles + at
+            pair = cols_ref[row, slot] + base
+            owned = (pair >= row * col_tiles) & (pair < (row + 1) * col_tiles) & (slot < count)
+            list_ref[live] = pair
             live = live + jnp.where(owned, 1, 0)
     list_ref[row_tiles * most] = live
-
-
-def row_kernel(list_ref, x_ref, y_ref, g_ref, lse_ref, columns, *sums):
-    col_tiles = y_ref.shape[0] // TILE
-    live = list_ref[list_ref.shape[0] - 1]
-    columns[...] = as_columns(split3(tile_rows(g_ref, col_tiles)))
+    copies[3].wait()
+    copies[4].wait()
     pick = lambda pair: (lax.rem(pair, col_tiles), lax.div(pair, col_tiles))
     lse_pass(list_ref, live, pick, y_ref, x_ref, col_tiles, columns, *sums)
     lse_finish(*sums[:2], lse_ref)
@@ -446,24 +470,27 @@
             pltpu.VMEM((LSE_GROUP, 8, TILE), f32),
         ]
 
-    pairs = pl.pallas_call(
-        functools.partial(list_kernel, col_tiles),
-        out_shape=jax.ShapeDtypeStruct((row_tiles * most + 1,), i32),
-        in_specs=[SMEM, SMEM],
-        out_specs=SMEM,
-        compiler_params=params(),
-        name="list_pairs",
-    )(tile_cols, tile_counts)
-
-    row_lse = pl.pallas_call(
+    sources = (tile_cols, tile_counts, g_init.reshape(col_shape), points_y, points_x)
+    row_lse, pairs, points_x, points_y = pl.pallas_call(
         row_kernel,
-        out_shape=jax.ShapeDtypeStruct(row_shape, f32),
-        in_specs=[SMEM, VMEM, VMEM, VMEM],
-        out_specs=VMEM,
-        scratch_shapes=lse_scratch(row_tiles),
+        out_shape=(
+            pltpu.VMEM(row_shape, f32),
+            jax.ShapeDtypeStruct((row_tiles * most + 1,), i32),
+            pltpu.VMEM(points_x.shape, bf16),
+            pltpu.VMEM(points_y.shape, bf16),
+        ),
+        in_specs=[HBM] * 5,
+        out_specs=(VMEM, SMEM, VMEM, VMEM),
+        scratch_shapes=[
+            pltpu.SMEM(tile_cols.shape, i32),
+            pltpu.SMEM(tile_counts.shape, i32),
+            pltpu.VMEM(col_shape, f32),
+            dma((5,)),
+        ]
+        + lse_scratch(row_tiles),
         compiler_params=params(),
         name="row_pass",
-    )(pairs, points_x, points_y, g_init.reshape(col_shape))
+    )(*[pltpu.with_memory_space_constraint(source, pltpu.HBM) for source in sources])
 
     f_pot = pl.pallas_call(
         functools.partial(row_join_kernel, gy_size),

time: 80.3 us -> 75.3 us (0.938)
  local copies, waits for them, and re-layouts: 6.24 us -> 1.33 us
    unnamed x17 -> x5, local copies, waits for them, and re-layouts: 6.24 us -> 1.33 us
    pallas_call x1, Pallas kernels: 20.2 us -> 21.6 us  [local(): pl.pallas_call(functools.partial(col_join_kernel, nz, ny), out_shape=jax....]
    pallas_call x1, Pallas kernels: 2.85 us -> 1.82 us  [local(): pl.pallas_call(bary_kernel, out_shape=(jax.ShapeDtypeStruct((row_tiles +...]
    pallas_call x1, Pallas kernels: 13.8 us -> 14.7 us  [local(): pl.pallas_call(functools.partial(row_join_kernel, gy_size), out_shape=jax...]
    pallas_call x2 -> x1, Pallas kernels: 4.27 us -> 3.87 us  [local(): pl.pallas_call(row_kernel, out_shape=(pltpu.VMEM(row_shape, f32), jax.Sha...]
where the time goes in v3:
time: 75.3 us; the launch traced here: 75.1 us
  Pallas kernels  73 us (97%)
  local copies, waits for them, and re-layouts  1.33 us (2%)
    pallas_call x1, Pallas kernels, local(): pl.pallas_call(functools.partial(bary_join_kernel, gy_size), out_shape=ja...  28.8 us
    pallas_call x1, Pallas kernels, local(): pl.pallas_call(functools.partial(col_join_kernel, nz, ny), out_shape=jax....  21.6 us
    pallas_call x1, Pallas kernels, local(): pl.pallas_call(functools.partial(row_join_kernel, gy_size), out_shape=jax...  14.7 us
    pallas_call x1, Pallas kernels, local(): pl.pallas_call(row_kernel, out_shape=(pltpu.VMEM(row_shape, f32), jax.Sha...  3.87 us
    pallas_call x1, Pallas kernels, local(): pl.pallas_call(column_kernel, out_shape=jax.ShapeDtypeStruct(col_shape, f...  2.18 us
    pallas_call x1, Pallas kernels, local(): pl.pallas_call(bary_kernel, out_shape=(jax.ShapeDtypeStruct((row_tiles +...  1.82 us

profile of v3, /device:TPU:1, one launch (start us, length us, event | category | flops | bytes accessed | tf_op | source)
XLA Modules:
  0.0 75.1 jit_solution(1471488875898873236)
XLA Ops:
  0.6 0.0 copy-start.1
  0.6 3.9 %row_pass.1 = (f32[32,128]{1,0:T(8,128)S(1)}, s32[129]{0:T(256)S(1)}, bf16[4096,128]{1,0:T(8,128)(2,1)S(1)}, bf16[8192,128]{1,0:T(8,128)(2,1)S(1)}) custom-call(s32[8,16]{1,0:T(8,128)} %cols_hbm.1, s32[8]{0:T(128)} %counts_hbm.1, f32[64,128]{1,0:T(8,128)} %bitcast.7, bf16[8192,128]{1,0:T(8,128)(2,1)} %y_hbm.1, bf16[4096,128]{1,0:T(8,128)(2,1)} %x_hbm.1), custom_call_target="tpu_custom_call" | custom-call | tf_op jit(solution)/shard_map/row_pass/pallas_call | solution.py:474
  4.5 0.0 copy-start
  4.5 0.0 copy-done.1
  4.5 14.7 %row_join.1.f_ref = f32[32,128]{1,0:T(8,128)S(1)} custom-call(f32[32,128]{1,0:T(8,128)S(1)} %get-tuple-element.13.lse_ref, f32[32,128]{1,0:T(8,128)S(1)} %bitcast.6), custom_call_target="tpu_custom_call" | custom-call | tf_op jit(solution)/shard_map/row_join/pallas_call | solution.py:495
  19.3 2.2 %column_pass.1.lse_ref = f32[64,128]{1,0:T(8,128)S(1)} custom-call(s32[129]{0:T(256)S(1)} %get-tuple-element.10.list_ref, bf16[4096,128]{1,0:T(8,128)(2,1)S(1)} %get-tuple-element.11.x_ref, bf16[8192,128]{1,0:T(8,128)(2,1)S(1)} %get-tuple-element.12.y_ref, f32[32,128]{1,0:T(8,128)S(1)} %row_join.1.f_ref), custom_call_target="tpu_custom_call" | custom-call | tf_op jit(solution)/shard_map/column_pass/pallas_call | solution.py:509
  21.4 0.0 copy-done
  21.5 21.6 %column_join.1.g_ref = f32[64,128]{1,0:T(8,128)S(1)} custom-call(f32[64,128]{1,0:T(8,128)S(1)} %column_pass.1.lse_ref, f32[64,128]{1,0:T(8,128)S(1)} %bitcast.5), custom_call_target="tpu_custom_call" | custom-call | tf_op jit(solution)/shard_map/column_join/pallas_call | solution.py:520
  43.1 1.8 %bary_pass.1 = (f32[9,136,512]{2,1,0:T(8,128)S(1)}, f32[32,128]{1,0:T(8,128)}, f32[64,128]{1,0:T(8,128)}) custom-call(s32[129]{0:T(256)S(1)} %get-tuple-element.10.list_ref, bf16[4096,128]{1,0:T(8,128)(2,1)S(1)} %get-tuple-element.11.x_ref, bf16[8192,128]{1,0:T(8,128)(2,1)S(1)} %get-tuple-element.12.y_ref, f32[32,128]{1,0:T(8,128)S(1)} %row_join.1.f_ref, ...), custom_call_target="tpu_custom_call" | custom-call | tf_op jit(solution)/shard_map/bary_pass/pallas_call | solution.py:535
  44.9 28.8 %bary_join.1 = f32[4096,128]{1,0:T(8,128)S(1)} custom-call(f32[9,136,512]{2,1,0:T(8,128)S(1)} %get-tuple-element.16.part_ref), custom_call_target="tpu_custom_call" | custom-call | tf_op jit(solution)/shard_map/bary_join/pallas_call | solution.py:554
  73.8 1.3 %copy.11 = f32[4096,128]{1,0:T(8,128)} copy(f32[4096,128]{1,0:T(8,128)S(1)} %bary_join.1) | data formatting | bytes 4194304
Async XLA Ops:
  0.6 3.9 %copy-start.1 = (f32[4096]{0:T(1024)S(1)}, f32[4096]{0:T(1024)}, u32[]{:S(2)}) copy-start(f32[4096]{0:T(1024)} %param.10) | copy-start | bytes 49156
  4.5 16.9 %copy-start = (f32[8192]{0:T(1024)S(1)}, f32[8192]{0:T(1024)}, u32[]{:S(2)}) copy-start(f32[8192]{0:T(1024)} %param.11) | copy-start | bytes 98308

commit v4 on v3

--- a/solution.py
+++ b/solution.py
@@ -11,8 +11,11 @@
 LANES = 128
 CHUNKS = TILE // LANES
 LSE_GROUP = 2
-BARY_GROUP = 3
+BARY_GROUP = 2
 PIECES = 4
+PIECE = TILE // PIECES
+PIECE_LANES = [slice(k * PIECE, (k + 1) * PIECE) for k in range(PIECES)]
+SLOTS = 2
 MESH = pl.DeviceIdType.MESH
 NEG_FILL = -1e30
 SCALE = 2.8853900817779268
@@ -161,6 +164,9 @@
     x_hbm,
     lse_ref,
     list_ref,
+    rest_ref,
+    slot_ref,
+    bias_ref,
     x_ref,
     y_ref,
     cols_ref,
@@ -183,16 +189,26 @@
     for copy in copies[:3]:
         copy.wait()
     columns[...] = as_columns(split3(tile_rows(g_ref, col_tiles)))
-    live = jnp.int32(0)
+    live, others = jnp.int32(0), jnp.int32(0)
     for row in range(row_tiles):
         count = counts_ref[row]
         base = (row - me) * col_tiles
+        first = live
         for slot in range(most):
             pair = cols_ref[row, slot] + base
             owned = (pair >= row * col_tiles) & (pair < (row + 1) * col_tiles) & (slot < count)
             list_ref[live] = pair
+            if slot >= SLOTS:
+                rest_ref[others] = pair
+                others = others + jnp.where(owned & (live - first >= SLOTS), 1, 0)
             live = live + jnp.where(owned, 1, 0)
-    list_ref[row_tiles * most] = live
+        for slot in range(SLOTS):
+            here = first + slot < live
+            pair = list_ref[first + slot]
+            slot_ref[row * SLOTS + slot] = jnp.where(here, pair - row * col_tiles, 0)
+            bias_ref[row * SLOTS + slot] = jnp.where(here, 0.0, NEG_FILL)
+    list_ref[row_tiles * most + SLOTS] = live
+    rest_ref[row_tiles * most] = others
     copies[3].wait()
     copies[4].wait()
     pick = lambda pair: (lax.rem(pair, col_tiles), lax.div(pair, col_tiles))
@@ -208,6 +224,29 @@
     pick = lambda pair: (lax.div(pair, col_tiles), lax.rem(pair, col_tiles))
     lse_pass(list_ref, live, pick, x_ref, y_ref, row_tiles, columns, *sums)
     lse_finish(*sums[:2], lse_ref)
+
+
+def bary_potentials(f_ref, g_ref, row_tiles, col_tiles, columns, pots_g, pots_f):
+    first = 3 * col_tiles
+    pots = split3(tile_rows(g_ref, col_tiles)) + split3(tile_rows(f_ref, row_tiles))
+    columns[...] = as_columns(pots)
+    lane = lax.broadcasted_iota(jnp.int32, (1, LANES), 1)
+    pots_g[...] = columns[...] * spread(jnp.where(lane < first, 1.0, 0.0))
+    pots_f[...] = columns[...] * spread(jnp.where(lane < first, 0.0, 1.0)) + spread(
+        jnp.where(lane == first + 3 * row_tiles, 1.0, 0.0)
+    )
+
+
+def bary_sums(x_tile, y_tile, pots_g, pots_f, row_mask, col_mask):
+    left = jnp.concatenate([y_tile, pots_g[...] + spread(row_mask)], axis=1)
+    right = jnp.concatenate([x_tile, pots_f[...] + spread(col_mask)], axis=1)
+    return product(left, right)
+
+
+def weighted(points, weights):
+    return lax.dot_general(
+        points, weights, (((0,), (0,)), ((), ())), preferred_element_type=jnp.float32
+    )
 
 
 def bary_kernel(
@@ -236,37 +275,27 @@
     col_tiles = y_ref.shape[0] // TILE
     width = x_ref.shape[1]
     live = list_ref[list_ref.shape[0] - 1]
-    first = 3 * col_tiles
-    pots = split3(tile_rows(g_ref, col_tiles)) + split3(tile_rows(f_ref, row_tiles))
-    columns[...] = as_columns(pots)
+    bary_potentials(f_ref, g_ref, row_tiles, col_tiles, columns, pots_g, pots_f)
     out_ref[...] = jnp.zeros_like(out_ref)
-
     spare = out_ref.shape[0] - 1
-    lane = lax.broadcasted_iota(jnp.int32, (1, LANES), 1)
-    of_g = spread(jnp.where(lane < first, 1.0, 0.0))
-    of_f = spread(jnp.where(lane < first, 0.0, 1.0))
-    pots_g[...] = columns[...] * of_g
-    pots_f[...] = columns[...] * of_f
     pick = lambda pair: (lax.div(pair, col_tiles), lax.rem(pair, col_tiles))
 
     def fill(group):
         for u in range(BARY_GROUP):
             row, col = pick(pair_at(list_ref, live, group * BARY_GROUP + u))
-            left = jnp.concatenate(
-                [tile_at(y_ref, col), pots_g[...] + spread(lane_mask(first, row_tiles, row))],
-                axis=1,
-            )
-            right = jnp.concatenate(
-                [tile_at(x_ref, row), pots_f[...] + spread(lane_mask(0, col_tiles, col))], axis=1
-            )
-            sums[u] = product(left, right)
+            row_mask = lane_mask(3 * col_tiles, row_tiles, row)
+            col_mask = lane_mask(0, col_tiles, col)
+            x_tile, y_tile = tile_at(x_ref, row), tile_at(y_ref, col)
+            sums[u] = bary_sums(x_tile, y_tile, pots_g, pots_f, row_mask, col_mask)
 
     def drain(group):
         for u in range(BARY_GROUP):
             at = group * BARY_GROUP + u
             row = jnp.where(at < live, pick(pair_at(list_ref, live, at))[0], spare)
             weights = jnp.exp2(sums[u] * SCALE)
-            out_ref[row, width:] += fold_rows(weights, jnp.sum)
+            mass = fold_rows(weights, jnp.sum)
+            for k, lanes in enumerate(PIECE_LANES):
+                out_ref[row, k, width:] += mass[:, lanes]
             rounded[u] = weights.astype(jnp.bfloat16)
 
     def add(group):
@@ -274,12 +303,9 @@
             at = group * BARY_GROUP + u
             row, col = pick(pair_at(list_ref, live, at))
             row = jnp.where(at < live, row, spare)
-            out_ref[row, :width] += lax.dot_general(
-                tile_at(y_ref, col),
-                rounded[u],
-                (((0,), (0,)), ((), ())),
-                preferred_element_type=jnp.float32,
-            )
+            total = weighted(tile_at(y_ref, col), rounded[u])
+            for k, lanes in enumerate(PIECE_LANES):
+                out_ref[row, k, :width] += total[:, lanes]
 
     pipelined(BARY_GROUP, live, fill, drain, add)
     for copy in results:
@@ -360,18 +386,80 @@
                 g_ref[rows] = 0.5 * (log_b_ref[rows] - joined)
 
 
-def bary_join_kernel(n, part_ref, out_ref, near, relay, left_in, right_in, sems):
+def bary_join_kernel(
+    n,
+    slot_ref,
+    bias_ref,
+    x_ref,
+    y_ref,
+    f_ref,
+    g_ref,
+    part_ref,
+    out_ref,
+    columns,
+    pots_g,
+    pots_f,
+    masks,
+    sums,
+    rounded,
+    whole,
+    near,
+    relay,
+    left_in,
+    right_in,
+    sems,
+):
     me = lax.axis_index("gy")
     chips = n // 2
     chip, core = lax.div(me, 2), lax.rem(me, 2)
     other = 1 - core
     width = out_ref.shape[1]
+    row_tiles, col_tiles = x_ref.shape[0] // TILE, y_ref.shape[0]
     split = width // 2
     low, high = slice(0, split), slice(split, width + 8)
     places = [lax.rem(chip + d, chips) for d in range(chips)]
     sibling = {"gy": chip * 2 + other}
     right, left = {"gy": places[1] * 2 + core}, {"gy": places[3] * 2 + core}
-    meet([sibling, right, left])
+    barrier = pltpu.get_barrier_semaphore()
+    for peer in (sibling, right, left):
+        pl.semaphore_signal(barrier, inc=1, device_id=peer, device_id_type=MESH)
+    bary_potentials(f_ref, g_ref, row_tiles, col_tiles, columns, pots_g, pots_f)
+
+    lane = lax.broadcasted_iota(jnp.int32, (1, LANES), 1)
+    bias_lane = jnp.where(lane == 3 * (col_tiles + row_tiles), 1.0, 0.0)
+    for col in range(col_tiles):
+        masks[col] = lane_mask(0, col_tiles, col)
+
+    def take(rows):
+        cols = []
+        for i, row in enumerate(rows):
+            row_mask = lane_mask(3 * col_tiles, row_tiles, row)
+            for k in range(SLOTS):
+                col = slot_ref[row * SLOTS + k]
+                cols.append(col)
+                sums[i * SLOTS + k] = bary_sums(
+                    tile_at(x_ref, row),
+                    y_ref[col],
+                    pots_g,
+                    pots_f,
+                    row_mask + bias_lane * bias_ref[row * SLOTS + k],
+                    masks[col],
+                )
+        for i, row in enumerate(rows):
+            mass = 0.0
+            for k in range(i * SLOTS, (i + 1) * SLOTS):
+                weights = jnp.exp2(sums[k] * SCALE)
+                mass = mass + fold_rows(weights, jnp.sum)
+                rounded[k] = weights.astype(jnp.bfloat16)
+            for k, lanes in enumerate(PIECE_LANES):
+                whole[row, k, width:] = part_ref[row, k, width:] + mass[:, lanes]
+        for i, row in enumerate(rows):
+            total = 0.0
+            for k in range(i * SLOTS, (i + 1) * SLOTS):
+                total = total + weighted(y_ref[cols[k]], rounded[k])
+            for k, lanes in enumerate(PIECE_LANES):
+                whole[row, k, :width] = part_ref[row, k, :width] + total[:, lanes]
+
     used = [0]
 
     def go(src, dst, peer):
@@ -379,42 +467,63 @@
         used[0] += 1
         return send(src, dst, sems.at[0, k], sems.at[1, k], peer)
 
-    pieces = [slice(k * TILE // PIECES, (k + 1) * TILE // PIECES) for k in range(PIECES)]
-    inside = {d: go(part_ref.at[places[d] * 2 + other], near.at[d], sibling) for d in (2, 1, 3, 0)}
-    waits = []
+    def tile(d, kind):
+        return places[d] * 2 + kind
+
+    pieces = list(range(PIECES))
+    inside, waits = {}, []
+
+    def give_inside(d):
+        inside[d] = go(whole.at[tile(d, other)], near.at[d], sibling)
 
     def add_inside(d):
         inside[d].wait()
-        near[d] = near[d] + part_ref[places[d] * 2 + core]
-
+        near[d] = near[d] + whole[tile(d, core)]
+
+    take([tile(2, other)])
+    pl.semaphore_wait(barrier, 3)
+    give_inside(2)
+    take([tile(2, core)])
     add_inside(2)
     far = []
     for piece in pieces:
         far.append(
             (
-                go(near.at[2, low, piece], relay.at[low, piece], right),
-                go(near.at[2, high, piece], relay.at[high, piece], left),
+                go(near.at[2, piece, low], relay.at[piece, low], right),
+                go(near.at[2, piece, high], relay.at[piece, high], left),
             )
         )
+    take([tile(1, other), tile(3, other)])
+    give_inside(1)
+    give_inside(3)
+    take([tile(1, core), tile(3, core)])
     add_inside(1)
     add_inside(3)
     direct, passed = [], []
-    for k, piece in enumerate(pieces):
+
+    def give_direct(piece):
         direct.append(
             (
-                go(near.at[1, high, piece], left_in.at[high, piece], right),
-                go(near.at[3, low, piece], right_in.at[low, piece], left),
+                go(near.at[1, piece, high], left_in.at[piece, high], right),
+                go(near.at[3, piece, low], right_in.at[piece, low], left),
             )
         )
-        if k == 0:
-            add_inside(0)
+
+    for piece in pieces[:2]:
+        give_direct(piece)
+    take([tile(0, other), tile(0, core)])
+    give_inside(0)
+    for k, piece in enumerate(pieces):
         far[k][0].wait()
-        near[1, low, piece] = near[1, low, piece] + relay[low, piece]
-        to_right = go(near.at[1, low, piece], left_in.at[low, piece], right)
+        near[1, piece, low] = near[1, piece, low] + relay[piece, low]
+        to_right = go(near.at[1, piece, low], left_in.at[piece, low], right)
         far[k][1].wait()
-        near[3, high, piece] = near[3, high, piece] + relay[high, piece]
-        to_left = go(near.at[3, high, piece], right_in.at[high, piece], left)
+        near[3, piece, high] = near[3, piece, high] + relay[piece, high]
+        to_left = go(near.at[3, piece, high], right_in.at[piece, high], left)
         passed.append((to_right, to_left))
+        for ahead in pieces[k + 2 : k + 3]:
+            give_direct(ahead)
+    add_inside(0)
 
     def rows_of(place, kind, first, count):
         start = (place * 2 + kind) * TILE + first
@@ -425,7 +534,7 @@
     for k, piece in enumerate(pieces):
         for copy in direct[k] + passed[k]:
             copy.wait()
-        total = near[0, :, piece] + left_in[:, piece] + right_in[:, piece]
+        total = near[0, k] + left_in[k] + right_in[k]
         ratio = total[:width] / jnp.sum(total[width:], axis=0, keepdims=True)
         mine = rows_of(chip, core, k * size, size)
         mine[...] = ratio.T
@@ -471,16 +580,19 @@
         ]
 
     sources = (tile_cols, tile_counts, g_init.reshape(col_shape), points_y, points_x)
-    row_lse, pairs, points_x, points_y = pl.pallas_call(
+    row_lse, pairs, rest, slots, biases, points_x, points_y = pl.pallas_call(
         row_kernel,
         out_shape=(
             pltpu.VMEM(row_shape, f32),
+            jax.ShapeDtypeStruct((row_tiles * most + SLOTS + 1,), i32),
             jax.ShapeDtypeStruct((row_tiles * most + 1,), i32),
+            jax.ShapeDtypeStruct((row_tiles * SLOTS,), i32),
+            jax.ShapeDtypeStruct((row_tiles * SLOTS,), f32),
             pltpu.VMEM(points_x.shape, bf16),
             pltpu.VMEM(points_y.shape, bf16),
         ),
         in_specs=[HBM] * 5,
-        out_specs=(VMEM, SMEM, VMEM, VMEM),
+        out_specs=(VMEM, SMEM, SMEM, SMEM, SMEM, VMEM, VMEM),
         scratch_shapes=[
             pltpu.SMEM(tile_cols.shape, i32),
             pltpu.SMEM(tile_counts.shape, i32),
@@ -532,10 +644,10 @@
         name="column_join",
     )(col_lse, log_b.reshape(col_shape))
 
-    partial, f_pot, g_pot = pl.pallas_call(
+    partial, f_out, g_out = pl.pallas_call(
         bary_kernel,
         out_shape=(
-            jax.ShapeDtypeStruct((row_tiles + 1, width + 8, TILE), f32),
+            jax.ShapeDtypeStruct((row_tiles + 1, PIECES, width + 8, PIECE), f32),
             jax.ShapeDtypeStruct(row_shape, f32),
             jax.ShapeDtypeStruct(col_shape, f32),
         ),
@@ -549,20 +661,27 @@
         ],
         compiler_params=params(),
         name="bary_pass",
-    )(pairs, points_x, points_y, f_pot, g_pot)
+    )(rest, points_x, points_y, f_pot, g_pot)
 
     barycenter = pl.pallas_call(
         functools.partial(bary_join_kernel, gy_size),
         out_shape=jax.ShapeDtypeStruct((rows, width), f32),
-        in_specs=[VMEM],
+        in_specs=[SMEM] * 2 + [VMEM] * 5,
         out_specs=VMEM,
-        scratch_shapes=[pltpu.VMEM((4, width + 8, TILE), f32)]
-        + [pltpu.VMEM((width + 8, TILE), f32)] * 3
+        scratch_shapes=[pltpu.VMEM((TILE, LANES), bf16)] * 3
+        + [
+            pltpu.VMEM((col_tiles, 1, LANES), f32),
+            pltpu.VMEM((2 * SLOTS, TILE, TILE), f32),
+            pltpu.VMEM((2 * SLOTS, TILE, TILE), bf16),
+            pltpu.VMEM((row_tiles, PIECES, width + 8, PIECE), f32),
+            pltpu.VMEM((4, PIECES, width + 8, PIECE), f32),
+        ]
+        + [pltpu.VMEM((PIECES, width + 8, PIECE), f32)] * 3
         + [dma((2, 4 + 15 * PIECES))],
         compiler_params=params(collective_id=2, has_side_effects=True),
         name="bary_join",
-    )(partial)
-    return (f_pot.reshape(-1), g_pot.reshape(-1), barycenter)
+    )(slots, biases, points_x, points_y.reshape(col_tiles, TILE, width), f_pot, g_pot, partial)
+    return (f_out.reshape(-1), g_out.reshape(-1), barycenter)
 
 
 def solution(mesh):

time: 75.3 us -> 73.5 us (0.976)
  Pallas kernels: 73 us -> 71.2 us
    pallas_call x1, Pallas kernels: 21.6 us -> 19.1 us  [local(): pl.pallas_call(functools.partial(col_join_kernel, nz, ny), out_shape=jax....]
    pallas_call x1, Pallas kernels: 28.8 us -> 31.2 us  [local(): pl.pallas_call(functools.partial(bary_join_kernel, gy_size), out_shape=ja...]
    pallas_call x1, Pallas kernels: 14.7 us -> 13.7 us  [local(): pl.pallas_call(functools.partial(row_join_kernel, gy_size), out_shape=jax...]
where the time goes in v4:
time: 73.5 us; the launch traced here: 73.3 us
  Pallas kernels  71.2 us (97%)
  local copies, waits for them, and re-layouts  1.33 us (2%)
    pallas_call x1, Pallas kernels, local(): pl.pallas_call(functools.partial(bary_join_kernel, gy_size), out_shape=ja...  31.2 us
    pallas_call x1, Pallas kernels, local(): pl.pallas_call(functools.partial(col_join_kernel, nz, ny), out_shape=jax....  19.1 us
    pallas_call x1, Pallas kernels, local(): pl.pallas_call(functools.partial(row_join_kernel, gy_size), out_shape=jax...  13.7 us
    pallas_call x1, Pallas kernels, local(): pl.pallas_call(row_kernel, out_shape=(pltpu.VMEM(row_shape, f32), jax.Sha...  3.9 us
    pallas_call x1, Pallas kernels, local(): pl.pallas_call(column_kernel, out_shape=jax.ShapeDtypeStruct(col_shape, f...  2.18 us

profile of v4, /device:TPU:1, one launch (start us, length us, event | category | flops | bytes accessed | tf_op | source)
XLA Modules:
  0.0 73.3 jit_solution(2746240108753678727)
XLA Ops:
  0.6 0.0 copy-start.1
  0.6 3.9 %row_pass.1 = (f32[32,128]{1,0:T(8,128)S(1)}, s32[131]{0:T(256)S(1)}, s32[129]{0:T(256)S(1)}, s32[16]{0:T(128)S(1)}, f32[16]{0:T(128)S(1)}, /*index=5*/bf16[4096...) custom-call(s32[8,16]{1,0:T(8,128)} %cols_hbm.1, s32[8]{0:T(128)} %counts_hbm.1, f32[64,128]{1,0:T(8,128)} %bitcast.9, ...), custom_call_target="tpu_custom_call" | custom-call | tf_op jit(solution)/shard_map/row_pass/pallas_call | solution.py:583
  4.5 0.0 copy-start
  4.6 0.0 copy-done.1
  4.6 13.7 %row_join.1.f_ref = f32[32,128]{1,0:T(8,128)S(1)} custom-call(f32[32,128]{1,0:T(8,128)S(1)} %get-tuple-element.16.lse_ref, f32[32,128]{1,0:T(8,128)S(1)} %bitcast.8), custom_call_target="tpu_custom_call" | custom-call | tf_op jit(solution)/shard_map/row_join/pallas_call | solution.py:607
  18.2 2.2 %column_pass.1.lse_ref = f32[64,128]{1,0:T(8,128)S(1)} custom-call(s32[131]{0:T(256)S(1)} %get-tuple-element.17.list_ref, bf16[4096,128]{1,0:T(8,128)(2,1)S(1)} %get-tuple-element.14.x_ref, bf16[8192,128]{1,0:T(8,128)(2,1)S(1)} %get-tuple-element.15.y_ref, f32[32,128]{1,0:T(8,128)S(1)} %row_join.1.f_ref), custom_call_target="tpu_custom_call" | custom-call | tf_op jit(solution)/shard_map/column_pass/pallas_call | solution.py:621
  20.4 0.0 copy-done
  20.4 19.1 %column_join.1.g_ref = f32[64,128]{1,0:T(8,128)S(1)} custom-call(f32[64,128]{1,0:T(8,128)S(1)} %column_pass.1.lse_ref, f32[64,128]{1,0:T(8,128)S(1)} %bitcast.7), custom_call_target="tpu_custom_call" | custom-call | tf_op jit(solution)/shard_map/column_join/pallas_call | solution.py:632
  39.5 1.2 %bary_pass.1 = (f32[9,4,136,128]{3,2,1,0:T(8,128)S(1)}, f32[32,128]{1,0:T(8,128)}, f32[64,128]{1,0:T(8,128)}) custom-call(s32[129]{0:T(256)S(1)} %get-tuple-element.13.list_ref, bf16[4096,128]{1,0:T(8,128)(2,1)S(1)} %get-tuple-element.14.x_ref, bf16[8192,128]{1,0:T(8,128)(2,1)S(1)} %get-tuple-element.15.y_ref, f32[32,128]{1,0:T(8,128)S(1)} %row_join.1.f_ref, ...), custom_call_target="tpu_custom_call" | custom-call | tf_op jit(solution)/shard_map/bary_pass/pallas_call | solution.py:647
  40.7 31.2 %bary_join.1 = f32[4096,128]{1,0:T(8,128)S(1)} custom-call(s32[16]{0:T(128)S(1)} %get-tuple-element.20.slot_ref, f32[16]{0:T(128)S(1)} %get-tuple-element.21.bias_ref, bf16[4096,128]{1,0:T(8,128)(2,1)S(1)} %get-tuple-element.14.x_ref, bf16[16,512,128]{2,1,0:T(8,128)(2,1)S(1)} %bitcast.6, f32[32,128]{1,0:T(8,128)S(1)} %row_join.1.f_ref, ...), custom_call_target="tpu_custom_call" | custom-call | tf_op jit(solution)/shard_map/bary_join/pallas_call | solution.py:666
  72.0 1.3 %copy.11 = f32[4096,128]{1,0:T(8,128)} copy(f32[4096,128]{1,0:T(8,128)S(1)} %bary_join.1) | data formatting | bytes 4194304
Async XLA Ops:
  0.6 3.9 %copy-start.1 = (f32[4096]{0:T(1024)S(1)}, f32[4096]{0:T(1024)}, u32[]{:S(2)}) copy-start(f32[4096]{0:T(1024)} %param.10) | copy-start | bytes 49156
  4.5 15.9 %copy-start = (f32[8192]{0:T(1024)S(1)}, f32[8192]{0:T(1024)}, u32[]{:S(2)}) copy-start(f32[8192]{0:T(1024)} %param.11) | copy-start | bytes 98308

commit v5 on v4

--- a/solution.py
+++ b/solution.py
@@ -22,6 +22,7 @@
 VMEM = pl.BlockSpec(memory_space=pltpu.VMEM)
 SMEM = pl.BlockSpec(memory_space=pltpu.SMEM)
 HBM = pl.BlockSpec(memory_space=pltpu.HBM)
+ANY = pl.BlockSpec(memory_space=pl.ANY)
 VMEM_LIMIT = 40 * 1024 * 1024
 
 
@@ -163,12 +164,16 @@
     y_hbm,
     x_hbm,
     lse_ref,
+    list_any,
+    rest_any,
+    slot_any,
+    bias_any,
+    x_ref,
+    y_ref,
     list_ref,
     rest_ref,
     slot_ref,
     bias_ref,
-    x_ref,
-    y_ref,
     cols_ref,
     counts_ref,
     g_ref,
@@ -209,18 +214,30 @@
             bias_ref[row * SLOTS + slot] = jnp.where(here, 0.0, NEG_FILL)
     list_ref[row_tiles * most + SLOTS] = live
     rest_ref[row_tiles * most] = others
+    leaving = [(list_ref, list_any), (rest_ref, rest_any), (slot_ref, slot_any)]
+    leaving += [(bias_ref, bias_any)]
+    leaving = [
+        pltpu.make_async_copy(src, dst, sems.at[5 + i]) for i, (src, dst) in enumerate(leaving)
+    ]
+    for copy in leaving:
+        copy.start()
     copies[3].wait()
     copies[4].wait()
     pick = lambda pair: (lax.rem(pair, col_tiles), lax.div(pair, col_tiles))
     lse_pass(list_ref, live, pick, y_ref, x_ref, col_tiles, columns, *sums)
     lse_finish(*sums[:2], lse_ref)
-
-
-def column_kernel(list_ref, x_ref, y_ref, f_ref, lse_ref, columns, *sums):
+    for copy in leaving:
+        copy.wait()
+
+
+def column_kernel(list_any, x_ref, y_ref, f_ref, lse_ref, list_ref, sem, columns, *sums):
+    fetch = pltpu.make_async_copy(list_any, list_ref, sem)
+    fetch.start()
     row_tiles = x_ref.shape[0] // TILE
     col_tiles = y_ref.shape[0] // TILE
+    columns[...] = as_columns(split3(tile_rows(f_ref, row_tiles)))
+    fetch.wait()
     live = list_ref[list_ref.shape[0] - 1]
-    columns[...] = as_columns(split3(tile_rows(f_ref, row_tiles)))
     pick = lambda pair: (lax.div(pair, col_tiles), lax.rem(pair, col_tiles))
     lse_pass(list_ref, live, pick, x_ref, y_ref, row_tiles, columns, *sums)
     lse_finish(*sums[:2], lse_ref)
@@ -250,7 +267,7 @@
 
 
 def bary_kernel(
-    list_ref,
+    list_any,
     x_ref,
     y_ref,
     f_ref,
@@ -258,6 +275,7 @@
     out_ref,
     f_hbm,
     g_hbm,
+    list_ref,
     columns,
     pots_g,
     pots_f,
@@ -265,6 +283,8 @@
     rounded,
     sems,
 ):
+    fetch = pltpu.make_async_copy(list_any, list_ref, sems.at[2])
+    fetch.start()
     results = [
         pltpu.make_async_copy(f_ref, f_hbm, sems.at[0]),
         pltpu.make_async_copy(g_ref, g_hbm, sems.at[1]),
@@ -274,9 +294,10 @@
     row_tiles = x_ref.shape[0] // TILE
     col_tiles = y_ref.shape[0] // TILE
     width = x_ref.shape[1]
-    live = list_ref[list_ref.shape[0] - 1]
     bary_potentials(f_ref, g_ref, row_tiles, col_tiles, columns, pots_g, pots_f)
     out_ref[...] = jnp.zeros_like(out_ref)
+    fetch.wait()
+    live = list_ref[list_ref.shape[0] - 1]
     spare = out_ref.shape[0] - 1
     pick = lambda pair: (lax.div(pair, col_tiles), lax.rem(pair, col_tiles))
 
@@ -388,14 +409,17 @@
 
 def bary_join_kernel(
     n,
-    slot_ref,
-    bias_ref,
+    slot_any,
+    bias_any,
     x_ref,
     y_ref,
     f_ref,
     g_ref,
     part_ref,
     out_ref,
+    slot_ref,
+    bias_ref,
+    here,
     columns,
     pots_g,
     pots_f,
@@ -423,12 +447,19 @@
     barrier = pltpu.get_barrier_semaphore()
     for peer in (sibling, right, left):
         pl.semaphore_signal(barrier, inc=1, device_id=peer, device_id_type=MESH)
+    fetches = [
+        pltpu.make_async_copy(slot_any, slot_ref, here.at[0]),
+        pltpu.make_async_copy(bias_any, bias_ref, here.at[1]),
+    ]
+    for fetch in fetches:
+        fetch.start()
     bary_potentials(f_ref, g_ref, row_tiles, col_tiles, columns, pots_g, pots_f)
-
     lane = lax.broadcasted_iota(jnp.int32, (1, LANES), 1)
     bias_lane = jnp.where(lane == 3 * (col_tiles + row_tiles), 1.0, 0.0)
     for col in range(col_tiles):
         masks[col] = lane_mask(0, col_tiles, col)
+    for fetch in fetches:
+        fetch.wait()
 
     def take(rows):
         cols = []
@@ -580,24 +611,28 @@
         ]
 
     sources = (tile_cols, tile_counts, g_init.reshape(col_shape), points_y, points_x)
+    lists = (
+        ((row_tiles * most + SLOTS + 1,), i32),
+        ((row_tiles * most + 1,), i32),
+        ((row_tiles * SLOTS,), i32),
+        ((row_tiles * SLOTS,), f32),
+    )
     row_lse, pairs, rest, slots, biases, points_x, points_y = pl.pallas_call(
         row_kernel,
         out_shape=(
             pltpu.VMEM(row_shape, f32),
-            jax.ShapeDtypeStruct((row_tiles * most + SLOTS + 1,), i32),
-            jax.ShapeDtypeStruct((row_tiles * most + 1,), i32),
-            jax.ShapeDtypeStruct((row_tiles * SLOTS,), i32),
-            jax.ShapeDtypeStruct((row_tiles * SLOTS,), f32),
+            *[jax.ShapeDtypeStruct(*a) for a in lists],
             pltpu.VMEM(points_x.shape, bf16),
             pltpu.VMEM(points_y.shape, bf16),
         ),
         in_specs=[HBM] * 5,
-        out_specs=(VMEM, SMEM, SMEM, SMEM, SMEM, VMEM, VMEM),
-        scratch_shapes=[
+        out_specs=(VMEM, ANY, ANY, ANY, ANY, VMEM, VMEM),
+        scratch_shapes=[pltpu.SMEM(*a) for a in lists]
+        + [
             pltpu.SMEM(tile_cols.shape, i32),
             pltpu.SMEM(tile_counts.shape, i32),
             pltpu.VMEM(col_shape, f32),
-            dma((5,)),
+            dma((9,)),
         ]
         + lse_scratch(row_tiles),
         compiler_params=params(),
@@ -621,9 +656,9 @@
     col_lse = pl.pallas_call(
         column_kernel,
         out_shape=jax.ShapeDtypeStruct(col_shape, f32),
-        in_specs=[SMEM, VMEM, VMEM, VMEM],
+        in_specs=[ANY, VMEM, VMEM, VMEM],
         out_specs=VMEM,
-        scratch_shapes=lse_scratch(col_tiles),
+        scratch_shapes=[pltpu.SMEM(pairs.shape, i32), dma] + lse_scratch(col_tiles),
         compiler_params=params(),
         name="column_pass",
     )(pairs, points_x, points_y, f_pot)
@@ -651,13 +686,14 @@
             jax.ShapeDtypeStruct(row_shape, f32),
             jax.ShapeDtypeStruct(col_shape, f32),
         ),
-        in_specs=[SMEM, VMEM, VMEM, VMEM, VMEM],
+        in_specs=[ANY, VMEM, VMEM, VMEM, VMEM],
         out_specs=(VMEM, HBM, HBM),
-        scratch_shapes=[pltpu.VMEM((TILE, LANES), bf16)] * 3
+        scratch_shapes=[pltpu.SMEM(rest.shape, i32)]
+        + [pltpu.VMEM((TILE, LANES), bf16)] * 3
         + [
             pltpu.VMEM((BARY_GROUP, TILE, TILE), f32),
             pltpu.VMEM((BARY_GROUP, TILE, TILE), bf16),
-            dma((2,)),
+            dma((3,)),
         ],
         compiler_params=params(),
         name="bary_pass",
@@ -666,9 +702,10 @@
     barycenter = pl.pallas_call(
         functools.partial(bary_join_kernel, gy_size),
         out_shape=jax.ShapeDtypeStruct((rows, width), f32),
-        in_specs=[SMEM] * 2 + [VMEM] * 5,
+        in_specs=[ANY] * 2 + [VMEM] * 5,
         out_specs=VMEM,
-        scratch_shapes=[pltpu.VMEM((TILE, LANES), bf16)] * 3
+        scratch_shapes=[pltpu.SMEM(slots.shape, i32), pltpu.SMEM(slots.shape, f32), dma((2,))]
+        + [pltpu.VMEM((TILE, LANES), bf16)] * 3
         + [
             pltpu.VMEM((col_tiles, 1, LANES), f32),
             pltpu.VMEM((2 * SLOTS, TILE, TILE), f32),

time: 73.5 us -> 72.7 us (0.989)
  Pallas kernels: 71.2 us -> 70.4 us
    pallas_call x1, Pallas kernels: 31.2 us -> 25.5 us  [local(): pl.pallas_call(functools.partial(bary_join_kernel, gy_size), out_shape=ja...]
    pallas_call x1, Pallas kernels: 19.1 us -> 21.4 us  [local(): pl.pallas_call(functools.partial(col_join_kernel, nz, ny), out_shape=jax....]
    pallas_call x1, Pallas kernels: 13.7 us -> 11.6 us  [local(): pl.pallas_call(functools.partial(row_join_kernel, gy_size), out_shape=jax...]
    pallas_call x1, Pallas kernels: 2.18 us -> 4.17 us  [local(): pl.pallas_call(column_kernel, out_shape=jax.ShapeDtypeStruct(col_shape, f...]
    pallas_call x1, Pallas kernels: 3.9 us -> 5.58 us  [local(): pl.pallas_call(row_kernel, out_shape=(pltpu.VMEM(row_shape, f32), *[jax.S...]
    pallas_call x1, Pallas kernels: 1.19 us -> 2.19 us  [local(): pl.pallas_call(bary_kernel, out_shape=(jax.ShapeDtypeStruct((row_tiles +...]
where the time goes in v5:
time: 72.7 us; the launch traced here: 72.5 us
  Pallas kernels  70.4 us (97%)
  local copies, waits for them, and re-layouts  1.33 us (2%)
    pallas_call x1, Pallas kernels, local(): pl.pallas_call(functools.partial(bary_join_kernel, gy_size), out_shape=ja...  25.5 us
    pallas_call x1, Pallas kernels, local(): pl.pallas_call(functools.partial(col_join_kernel, nz, ny), out_shape=jax....  21.4 us
    pallas_call x1, Pallas kernels, local(): pl.pallas_call(functools.partial(row_join_kernel, gy_size), out_shape=jax...  11.6 us
    pallas_call x1, Pallas kernels, local(): pl.pallas_call(row_kernel, out_shape=(pltpu.VMEM(row_shape, f32), *[jax.S...  5.58 us
    pallas_call x1, Pallas kernels, local(): pl.pallas_call(column_kernel, out_shape=jax.ShapeDtypeStruct(col_shape, f...  4.17 us
    pallas_call x1, Pallas kernels, local(): pl.pallas_call(bary_kernel, out_shape=(jax.ShapeDtypeStruct((row_tiles +...  2.19 us

profile of v5, /device:TPU:1, one launch (start us, length us, event | category | flops | bytes accessed | tf_op | source)
XLA Modules:
  0.0 72.5 jit_solution(12436867440261164582)
XLA Ops:
  0.6 0.0 copy-start.1
  0.6 5.6 %row_pass.1 = (f32[32,128]{1,0:T(8,128)S(1)}, s32[131]{0:T(256)S(1)}, s32[129]{0:T(256)S(1)}, s32[16]{0:T(128)S(1)}, f32[16]{0:T(128)S(1)}, /*index=5*/bf16[4096...) custom-call(s32[8,16]{1,0:T(8,128)} %cols_hbm.1, s32[8]{0:T(128)} %counts_hbm.1, f32[64,128]{1,0:T(8,128)} %bitcast.9, ...), custom_call_target="tpu_custom_call" | custom-call | tf_op jit(solution)/shard_map/row_pass/pallas_call | solution.py:620
  6.2 0.0 copy-start
  6.2 0.0 copy-done.1
  6.3 11.6 %row_join.1.f_ref = f32[32,128]{1,0:T(8,128)S(1)} custom-call(f32[32,128]{1,0:T(8,128)S(1)} %get-tuple-element.16.lse_ref, f32[32,128]{1,0:T(8,128)S(1)} %bitcast.8), custom_call_target="tpu_custom_call" | custom-call | tf_op jit(solution)/shard_map/row_join/pallas_call | solution.py:642
  17.8 4.2 %column_pass.1.lse_ref = f32[64,128]{1,0:T(8,128)S(1)} custom-call(s32[131]{0:T(256)S(1)} %get-tuple-element.17.list_any, bf16[4096,128]{1,0:T(8,128)(2,1)S(1)} %get-tuple-element.14.x_ref, bf16[8192,128]{1,0:T(8,128)(2,1)S(1)} %get-tuple-element.15.y_ref, f32[32,128]{1,0:T(8,128)S(1)} %row_join.1.f_ref), custom_call_target="tpu_custom_call" | custom-call | tf_op jit(solution)/shard_map/column_pass/pallas_call | solution.py:656
  22.0 0.0 copy-done
  22.0 21.4 %column_join.1.g_ref = f32[64,128]{1,0:T(8,128)S(1)} custom-call(f32[64,128]{1,0:T(8,128)S(1)} %column_pass.1.lse_ref, f32[64,128]{1,0:T(8,128)S(1)} %bitcast.7), custom_call_target="tpu_custom_call" | custom-call | tf_op jit(solution)/shard_map/column_join/pallas_call | solution.py:667
  43.4 2.2 %bary_pass.1 = (f32[9,4,136,128]{3,2,1,0:T(8,128)S(1)}, f32[32,128]{1,0:T(8,128)}, f32[64,128]{1,0:T(8,128)}) custom-call(s32[129]{0:T(256)S(1)} %get-tuple-element.13.list_any, bf16[4096,128]{1,0:T(8,128)(2,1)S(1)} %get-tuple-element.14.x_ref, bf16[8192,128]{1,0:T(8,128)(2,1)S(1)} %get-tuple-element.15.y_ref, f32[32,128]{1,0:T(8,128)S(1)} %row_join.1.f_ref, ...), custom_call_target="tpu_custom_call" | custom-call | tf_op jit(solution)/shard_map/bary_pass/pallas_call | solution.py:682
  45.6 25.5 %bary_join.1 = f32[4096,128]{1,0:T(8,128)S(1)} custom-call(s32[16]{0:T(128)S(1)} %get-tuple-element.20.slot_any, f32[16]{0:T(128)S(1)} %get-tuple-element.21.bias_any, bf16[4096,128]{1,0:T(8,128)(2,1)S(1)} %get-tuple-element.14.x_ref, bf16[16,512,128]{2,1,0:T(8,128)(2,1)S(1)} %bitcast.6, f32[32,128]{1,0:T(8,128)S(1)} %row_join.1.f_ref, ...), custom_call_target="tpu_custom_call" | custom-call | tf_op jit(solution)/shard_map/bary_join/pallas_call | solution.py:702
  71.2 1.3 %copy.11 = f32[4096,128]{1,0:T(8,128)} copy(f32[4096,128]{1,0:T(8,128)S(1)} %bary_join.1) | data formatting | bytes 4194304
Async XLA Ops:
  0.6 5.6 %copy-start.1 = (f32[4096]{0:T(1024)S(1)}, f32[4096]{0:T(1024)}, u32[]{:S(2)}) copy-start(f32[4096]{0:T(1024)} %param.10) | copy-start | bytes 49156
  6.2 15.8 %copy-start = (f32[8192]{0:T(1024)S(1)}, f32[8192]{0:T(1024)}, u32[]{:S(2)}) copy-start(f32[8192]{0:T(1024)} %param.11) | copy-start | bytes 98308

commit v6 on v5

--- a/solution.py
+++ b/solution.py
@@ -163,7 +163,8 @@
     g_hbm,
     y_hbm,
     x_hbm,
-    lse_ref,
+    peak,
+    mass,
     list_any,
     rest_any,
     slot_any,
@@ -224,13 +225,14 @@
     copies[3].wait()
     copies[4].wait()
     pick = lambda pair: (lax.rem(pair, col_tiles), lax.div(pair, col_tiles))
-    lse_pass(list_ref, live, pick, y_ref, x_ref, col_tiles, columns, *sums)
-    lse_finish(*sums[:2], lse_ref)
+    lse_pass(list_ref, live, pick, y_ref, x_ref, col_tiles, columns, peak, mass, *sums)
     for copy in leaving:
         copy.wait()
 
 
-def column_kernel(list_any, x_ref, y_ref, f_ref, lse_ref, list_ref, sem, columns, *sums):
+def column_kernel(
+    list_any, x_ref, y_ref, f_ref, peak, mass, list_ref, sem, columns, *sums
+):
     fetch = pltpu.make_async_copy(list_any, list_ref, sem)
     fetch.start()
     row_tiles = x_ref.shape[0] // TILE
@@ -239,8 +241,7 @@
     fetch.wait()
     live = list_ref[list_ref.shape[0] - 1]
     pick = lambda pair: (lax.div(pair, col_tiles), lax.rem(pair, col_tiles))
-    lse_pass(list_ref, live, pick, x_ref, y_ref, row_tiles, columns, *sums)
-    lse_finish(*sums[:2], lse_ref)
+    lse_pass(list_ref, live, pick, x_ref, y_ref, row_tiles, columns, peak, mass, *sums)
 
 
 def bary_potentials(f_ref, g_ref, row_tiles, col_tiles, columns, pots_g, pots_f):
@@ -333,10 +334,11 @@
         copy.wait()
 
 
-def meet(peers):
+def meet(peers, work):
     barrier = pltpu.get_barrier_semaphore()
     for peer in peers:
         pl.semaphore_signal(barrier, inc=1, device_id=peer, device_id_type=MESH)
+    work()
     pl.semaphore_wait(barrier, len(peers))
 
 
@@ -363,48 +365,60 @@
     return top + jnp.log(total)
 
 
-def row_join_kernel(n, lse_ref, log_a_ref, f_ref, held, send_sem, recv_sem):
+def row_join_kernel(n, peak, mass, log_a_ref, f_ref, lse_ref, held, send_sem, recv_sem):
     me = lax.axis_index("gy")
     peers = [{"gy": lax.rem(me + d, n)} for d in range(1, n)]
-    meet(peers)
+    meet(peers, lambda: lse_finish(peak, mass, lse_ref))
     copies = [
         send(lse_ref, held.at[me], send_sem.at[i], recv_sem.at[i], peer)
         for i, peer in enumerate(peers)
     ]
     held[me] = lse_ref[...]
     for copy in copies:
-        copy.wait()
+        copy.wait_recv()
     f_ref[...] = 0.5 * (log_a_ref[...] - join([held[k] for k in range(n)]))
-
-
-def col_join_kernel(nz, ny, lse_ref, log_b_ref, g_ref, first, part, second, sems):
+    for copy in copies:
+        copy.wait_send()
+
+
+def col_join_kernel(
+    nz, ny, peak, mass, log_b_ref, g_ref, lse_ref, first, part, second, sems
+):
     me = lax.axis_index("gx")
     z, y = lax.div(me, ny), lax.rem(me, ny)
     y_peers = [{"gx": z * ny + lax.rem(y + d, ny)} for d in range(1, ny)]
     z_peers = [{"gx": lax.rem(z + d, nz) * ny + y} for d in range(1, nz)]
-    meet(y_peers + z_peers)
+    meet(y_peers + z_peers, lambda: lse_finish(peak, mass, lse_ref))
     half = lse_ref.shape[0] // 2
-    n = ny
-    for stage in range(2):
+    copies = []
+
+    def give(stage, upper):
         held = (first, second)[stage]
-        copies = []
-        for upper in range(2):
-            own = lse_ref.at[pl.ds(upper * half, half)] if stage == 0 else part.at[upper]
-            along_y = upper == stage
-            at = y if along_y else z
-            for i, peer in enumerate(y_peers if along_y else z_peers):
-                k = (stage * 2 + upper) * (n - 1) + i
-                copies.append(send(own, held.at[upper, at], sems.at[0, k], sems.at[1, k], peer))
-            held[upper, at] = own[...]
-        for copy in copies:
-            copy.wait()
-        for upper in range(2):
-            joined = join([held[upper, k] for k in range(n)])
-            if stage == 0:
-                part[upper] = joined
-            else:
-                rows = slice(upper * half, (upper + 1) * half)
-                g_ref[rows] = 0.5 * (log_b_ref[rows] - joined)
+        own = lse_ref.at[pl.ds(upper * half, half)] if stage == 0 else part.at[upper]
+        at, peers = (y, y_peers) if upper == stage else (z, z_peers)
+        given = []
+        for peer in peers:
+            k = len(copies)
+            copy = send(own, held.at[upper, at], sems.at[0, k], sems.at[1, k], peer)
+            copies.append(copy)
+            given.append(copy)
+        held[upper, at] = own[...]
+        return given
+
+    def joined(stage, upper, given):
+        for copy in given:
+            copy.wait_recv()
+        return join([(first, second)[stage][upper, k] for k in range(ny)])
+
+    given = [give(0, upper) for upper in range(2)]
+    for upper in range(2):
+        part[upper] = joined(0, upper, given[upper])
+        given[upper] = give(1, upper)
+    for upper in range(2):
+        rows = slice(upper * half, (upper + 1) * half)
+        g_ref[rows] = 0.5 * (log_b_ref[rows] - joined(1, upper, given[upper]))
+    for copy in copies:
+        copy.wait_send()
 
 
 def bary_join_kernel(
@@ -491,12 +505,14 @@
             for k, lanes in enumerate(PIECE_LANES):
                 whole[row, k, :width] = part_ref[row, k, :width] + total[:, lanes]
 
-    used = [0]
+    used, copies = [0], []
 
     def go(src, dst, peer):
         k = used[0]
         used[0] += 1
-        return send(src, dst, sems.at[0, k], sems.at[1, k], peer)
+        copy = send(src, dst, sems.at[0, k], sems.at[1, k], peer)
+        copies.append(copy)
+        return copy
 
     def tile(d, kind):
         return places[d] * 2 + kind
@@ -508,7 +524,7 @@
         inside[d] = go(whole.at[tile(d, other)], near.at[d], sibling)
 
     def add_inside(d):
-        inside[d].wait()
+        inside[d].wait_recv()
         near[d] = near[d] + whole[tile(d, core)]
 
     take([tile(2, other)])
@@ -545,10 +561,10 @@
     take([tile(0, other), tile(0, core)])
     give_inside(0)
     for k, piece in enumerate(pieces):
-        far[k][0].wait()
+        far[k][0].wait_recv()
         near[1, piece, low] = near[1, piece, low] + relay[piece, low]
         to_right = go(near.at[1, piece, low], left_in.at[piece, low], right)
-        far[k][1].wait()
+        far[k][1].wait_recv()
         near[3, piece, high] = near[3, piece, high] + relay[piece, high]
         to_left = go(near.at[3, piece, high], right_in.at[piece, high], left)
         passed.append((to_right, to_left))
@@ -564,7 +580,7 @@
     own = []
     for k, piece in enumerate(pieces):
         for copy in direct[k] + passed[k]:
-            copy.wait()
+            copy.wait_recv()
         total = near[0, k] + left_in[k] + right_in[k]
         ratio = total[:width] / jnp.sum(total[width:], axis=0, keepdims=True)
         mine = rows_of(chip, core, k * size, size)
@@ -574,18 +590,20 @@
     onward = []
     for k in range(PIECES):
         for side in range(2):
-            own[k][side].wait()
+            own[k][side].wait_recv()
             place = places[3] if side == 0 else places[1]
             block = rows_of(place, core, k * size + side * size // 2, size // 2)
             onward.append((k, side, go(block, block, right if side == 0 else left)))
             block = rows_of(place, core, k * size, size)
             waits.append(go(block, block, sibling))
     for k, side, copy in onward:
-        copy.wait()
+        copy.wait_recv()
         block = rows_of(places[2], core, k * size + side * size // 2, size // 2)
         waits.append(go(block, block, sibling))
     for copy in waits:
-        copy.wait()
+        copy.wait_recv()
+    for copy in copies:
+        copy.wait_send()
 
 
 def local(gx_size, gy_size, points_x, points_y, g_init, log_a, log_b, tile_cols, tile_counts):
@@ -601,14 +619,11 @@
     row_shape, col_shape = (rows // LANES, LANES), (cols // LANES, LANES)
     dma = pltpu.SemaphoreType.DMA
 
-    def lse_scratch(tiles):
-        return [
-            pltpu.VMEM((TILE, LANES), bf16),
-            pltpu.VMEM((tiles + 1, 8, TILE), f32),
-            pltpu.VMEM((tiles + 1, 8, TILE), f32),
-            pltpu.VMEM((LSE_GROUP, TILE, TILE), f32),
-            pltpu.VMEM((LSE_GROUP, 8, TILE), f32),
-        ]
+    lse_scratch = [
+        pltpu.VMEM((TILE, LANES), bf16),
+        pltpu.VMEM((LSE_GROUP, TILE, TILE), f32),
+        pltpu.VMEM((LSE_GROUP, 8, TILE), f32),
+    ]
 
     sources = (tile_cols, tile_counts, g_init.reshape(col_shape), points_y, points_x)
     lists = (
@@ -617,16 +632,16 @@
         ((row_tiles * SLOTS,), i32),
         ((row_tiles * SLOTS,), f32),
     )
-    row_lse, pairs, rest, slots, biases, points_x, points_y = pl.pallas_call(
+    row_peak, row_mass, pairs, rest, slots, biases, points_x, points_y = pl.pallas_call(
         row_kernel,
         out_shape=(
-            pltpu.VMEM(row_shape, f32),
+            *[pltpu.VMEM((row_tiles + 1, 8, TILE), f32)] * 2,
             *[jax.ShapeDtypeStruct(*a) for a in lists],
             pltpu.VMEM(points_x.shape, bf16),
             pltpu.VMEM(points_y.shape, bf16),
         ),
         in_specs=[HBM] * 5,
-        out_specs=(VMEM, ANY, ANY, ANY, ANY, VMEM, VMEM),
+        out_specs=(VMEM, VMEM, ANY, ANY, ANY, ANY, VMEM, VMEM),
         scratch_shapes=[pltpu.SMEM(*a) for a in lists]
         + [
             pltpu.SMEM(tile_cols.shape, i32),
@@ -634,7 +649,7 @@
             pltpu.VMEM(col_shape, f32),
             dma((9,)),
         ]
-        + lse_scratch(row_tiles),
+        + lse_scratch,
         compiler_params=params(),
         name="row_pass",
     )(*[pltpu.with_memory_space_constraint(source, pltpu.HBM) for source in sources])
@@ -642,23 +657,24 @@
     f_pot = pl.pallas_call(
         functools.partial(row_join_kernel, gy_size),
         out_shape=jax.ShapeDtypeStruct(row_shape, f32),
-        in_specs=[VMEM, VMEM],
+        in_specs=[VMEM] * 3,
         out_specs=VMEM,
         scratch_shapes=[
+            pltpu.VMEM(row_shape, f32),
             pltpu.VMEM((gy_size,) + row_shape, f32),
             dma((gy_size - 1,)),
             dma((gy_size - 1,)),
         ],
         compiler_params=params(collective_id=0, has_side_effects=True),
         name="row_join",
-    )(row_lse, log_a.reshape(row_shape))
-
-    col_lse = pl.pallas_call(
+    )(row_peak, row_mass, log_a.reshape(row_shape))
+
+    col_peak, col_mass = pl.pallas_call(
         column_kernel,
-        out_shape=jax.ShapeDtypeStruct(col_shape, f32),
+        out_shape=[pltpu.VMEM((col_tiles + 1, 8, TILE), f32)] * 2,
         in_specs=[ANY, VMEM, VMEM, VMEM],
-        out_specs=VMEM,
-        scratch_shapes=[pltpu.SMEM(pairs.shape, i32), dma] + lse_scratch(col_tiles),
+        out_specs=[VMEM] * 2,
+        scratch_shapes=[pltpu.SMEM(pairs.shape, i32), dma] + lse_scratch,
         compiler_params=params(),
         name="column_pass",
     )(pairs, points_x, points_y, f_pot)
@@ -667,9 +683,10 @@
     g_pot = pl.pallas_call(
         functools.partial(col_join_kernel, nz, ny),
         out_shape=jax.ShapeDtypeStruct(col_shape, f32),
-        in_specs=[VMEM, VMEM],
+        in_specs=[VMEM] * 3,
         out_specs=VMEM,
         scratch_shapes=[
+            pltpu.VMEM(col_shape, f32),
             pltpu.VMEM((2, ny) + half[1:], f32),
             pltpu.VMEM(half, f32),
             pltpu.VMEM((2, ny) + half[1:], f32),
@@ -677,7 +694,7 @@
         ],
         compiler_params=params(collective_id=1, has_side_effects=True),
         name="column_join",
-    )(col_lse, log_b.reshape(col_shape))
+    )(col_peak, col_mass, log_b.reshape(col_shape))
 
     partial, f_out, g_out = pl.pallas_call(
         bary_kernel,

time: 72.7 us -> 72.6 us (level)
    pallas_call x2, Pallas kernels: 9.75 us -> 7.38 us  [the longest x1 4.44 us: local(): pl.pallas_call(row_kernel, out_shape=(*[pltpu.VMEM((row_tiles + 1, 8, TIL...]
    pallas_call x1, Pallas kernels: 25.5 us -> 27.9 us  [local(): pl.pallas_call(functools.partial(bary_join_kernel, gy_size), out_shape=ja...]
    pallas_call x1, Pallas kernels: 2.19 us -> 0.78 us  [local(): pl.pallas_call(bary_kernel, out_shape=(jax.ShapeDtypeStruct((row_tiles +...]
    pallas_call x1, Pallas kernels: 11.6 us -> 12.6 us  [local(): pl.pallas_call(functools.partial(row_join_kernel, gy_size), out_shape=jax...]
where the time goes in v6:
time: 72.6 us; the launch traced here: 72.2 us
  Pallas kernels  70.1 us (97%)
  local copies, waits for them, and re-layouts  1.33 us (2%)
    pallas_call x1, Pallas kernels, local(): pl.pallas_call(functools.partial(bary_join_kernel, gy_size), out_shape=ja...  27.9 us
    pallas_call x1, Pallas kernels, local(): pl.pallas_call(functools.partial(col_join_kernel, nz, ny), out_shape=jax....  21.5 us
    pallas_call x1, Pallas kernels, local(): pl.pallas_call(functools.partial(row_join_kernel, gy_size), out_shape=jax...  12.6 us
    pallas_call x1, Pallas kernels, local(): pl.pallas_call(row_kernel, out_shape=(*[pltpu.VMEM((row_tiles + 1, 8, TIL...  4.44 us
    pallas_call x1, Pallas kernels, local(): pl.pallas_call(column_kernel, out_shape=[pltpu.VMEM((col_tiles + 1, 8, TI...  2.94 us

profile of v6, /device:TPU:1, one launch (start us, length us, event | category | flops | bytes accessed | tf_op | source)
XLA Modules:
  0.0 72.2 jit_solution(12985722521165057706)
XLA Ops:
  0.6 0.0 copy-start.1
  0.6 4.4 %row_pass.1 = (f32[9,8,512]{2,1,0:T(8,128)S(1)}, f32[9,8,512]{2,1,0:T(8,128)S(1)}, s32[131]{0:T(256)S(1)}, s32[129]{0:T(256)S(1)}, s32[16]{0:T(128)S(1)}, /*inde...) custom-call(s32[8,16]{1,0:T(8,128)} %cols_hbm.1, s32[8]{0:T(128)} %counts_hbm.1, ...), custom_call_target="tpu_custom_call" | custom-call | tf_op jit(solution)/shard_map/row_pass/pallas_call | solution.py:635
  5.1 0.0 copy-start
  5.1 0.0 copy-done.1
  5.1 12.6 %row_join.1.f_ref = f32[32,128]{1,0:T(8,128)S(1)} custom-call(f32[9,8,512]{2,1,0:T(8,128)S(1)} %get-tuple-element.19.peak, f32[9,8,512]{2,1,0:T(8,128)S(1)} %get-tuple-element.20.mass, f32[32,128]{1,0:T(8,128)S(1)} %bitcast.8), custom_call_target="tpu_custom_call" | custom-call | tf_op jit(solution)/shard_map/row_join/pallas_call | solution.py:657
  17.7 2.9 %column_pass.1 = (f32[17,8,512]{2,1,0:T(8,128)S(1)}, f32[17,8,512]{2,1,0:T(8,128)S(1)}) custom-call(s32[131]{0:T(256)S(1)} %get-tuple-element.21.list_any, bf16[4096,128]{1,0:T(8,128)(2,1)S(1)} %get-tuple-element.17.x_ref, bf16[8192,128]{1,0:T(8,128)(2,1)S(1)} %get-tuple-element.18.y_ref, f32[32,128]{1,0:T(8,128)S(1)} %row_join.1.f_ref), custom_call_target="tpu_custom_call" | custom-call | tf_op jit(solution)/shard_map/column_pass/pallas_call | solution.py:672
  20.7 0.0 copy-done
  20.7 21.5 %column_join.1.g_ref = f32[64,128]{1,0:T(8,128)S(1)} custom-call(f32[17,8,512]{2,1,0:T(8,128)S(1)} %get-tuple-element.22.peak, f32[17,8,512]{2,1,0:T(8,128)S(1)} %get-tuple-element.23.mass, f32[64,128]{1,0:T(8,128)S(1)} %bitcast.7), custom_call_target="tpu_custom_call" | custom-call | tf_op jit(solution)/shard_map/column_join/pallas_call | solution.py:683
  42.2 0.8 %bary_pass.1 = (f32[9,4,136,128]{3,2,1,0:T(8,128)S(1)}, f32[32,128]{1,0:T(8,128)}, f32[64,128]{1,0:T(8,128)}) custom-call(s32[129]{0:T(256)S(1)} %get-tuple-element.16.list_any, bf16[4096,128]{1,0:T(8,128)(2,1)S(1)} %get-tuple-element.17.x_ref, bf16[8192,128]{1,0:T(8,128)(2,1)S(1)} %get-tuple-element.18.y_ref, f32[32,128]{1,0:T(8,128)S(1)} %row_join.1.f_ref, ...), custom_call_target="tpu_custom_call" | custom-call | tf_op jit(solution)/shard_map/bary_pass/pallas_call | solution.py:699
  43.0 27.9 %bary_join.1 = f32[4096,128]{1,0:T(8,128)S(1)} custom-call(s32[16]{0:T(128)S(1)} %get-tuple-element.26.slot_any, f32[16]{0:T(128)S(1)} %get-tuple-element.27.bias_any, bf16[4096,128]{1,0:T(8,128)(2,1)S(1)} %get-tuple-element.17.x_ref, bf16[16,512,128]{2,1,0:T(8,128)(2,1)S(1)} %bitcast.6, f32[32,128]{1,0:T(8,128)S(1)} %row_join.1.f_ref, ...), custom_call_target="tpu_custom_call" | custom-call | tf_op jit(solution)/shard_map/bary_join/pallas_call | solution.py:719
  70.8 1.3 %copy.11 = f32[4096,128]{1,0:T(8,128)} copy(f32[4096,128]{1,0:T(8,128)S(1)} %bary_join.1) | data formatting | bytes 4194304
Async XLA Ops:
  0.6 4.5 %copy-start.1 = (f32[4096]{0:T(1024)S(1)}, f32[4096]{0:T(1024)}, u32[]{:S(2)}) copy-start(f32[4096]{0:T(1024)} %param.10) | copy-start | bytes 49156
  5.1 15.6 %copy-start = (f32[8192]{0:T(1024)S(1)}, f32[8192]{0:T(1024)}, u32[]{:S(2)}) copy-start(f32[8192]{0:T(1024)} %param.11) | copy-start | bytes 98308
